TPU v7x, 512 devices: a whole 4x8x8 slice. The times are simulated.
512 devices in a mesh: rows: 64 (over x, y, core), grp: 8 (over z).
Axes of the slice: x: 4, y: 8, z: 8, core: 2. Of those that a mesh axis runs over, the one named last changes fastest.
Arguments:
- a_blocks: bfloat16 [24576, 64, 512], P(('rows', 'grp')), may hold values from -1 to 1
- prolong: bfloat16 [24576, 64, 128], P(('rows', 'grp')), may hold values from -1 to 1
- a_cols: int32 [24576, 8], P(('rows', 'grp')), may hold values from -1 to 55, as said below
- read_slots: int32 [1024, 4], P(('rows', 'grp')), may hold values from -1 to 47, as said below
- agg: int32 [24576], P(('rows', 'grp')), may hold values from 0 to 7
- rap_slot: int32 [24576, 8], P(('rows', 'grp')), may hold values from 0 to 7
Outputs:
- coarse_op: float32 [512, 8, 16384], P(('rows', 'grp'))
Inputs may be any that keep to these rules, and one draw needn't show every extreme that they name: `a_cols`: slot 0 of every row is the row itself; an entry of 48 or more names a read-list entry that is not -1. `read_slots`: the entries of one list that are not -1 come first and are distinct; devices at the ends of rows have only -1 toward the missing side.
All inputs are finite; a program needn't handle non-finite values.
Results may differ from a plain program's by a relative error of at most 0.009.
Values may be sent and summed in bfloat16 or wider, within the bound.
A program may use at most 128 MiB of HBM per device.

v0:
```python
import jax
import jax.numpy as jnp
from jax import lax
from jax.sharding import PartitionSpec as P

CSLOT = 8
NC_DEV = 1


def from_behind(value, axis, steps):
    count = lax.axis_size(axis)
    first, last = (max(0, -steps), min(count, count - steps))
    return lax.ppermute(value, axis, [(source, source + steps) for source in range(first, last)])


def select_blocks(source, wanted):
    chosen = source[jnp.maximum(wanted - 1, 0)]
    return jnp.where((wanted > 0)[..., None, None], chosen, 0)


def on_device(a_blocks, prolong, a_cols, read_slots, agg, rap_slot):
    shard_rows, block_cells, wide_cols = a_blocks.shape
    coarse_cols = prolong.shape[2]
    slot_count = a_cols.shape[1]
    requests = read_slots + 1
    pieces = []
    for side, offset in ((0, -1), (1, 1)):
        wanted = from_behind(requests[side], "rows", offset)
        pieces.append(from_behind(select_blocks(prolong, wanted), "rows", -offset))
    received = jnp.concatenate(pieces, axis=0)
    buffer = jnp.concatenate([prolong, received], axis=0)
    live = a_cols >= 0
    columns = buffer[jnp.maximum(a_cols, 0)]
    blocks = a_blocks.reshape(shard_rows, block_cells, slot_count, block_cells)
    panel_rows = lax.axis_size("grp") * NC_DEV
    target_count = panel_rows * CSLOT
    near = jnp.einsum("iakb,ikbc->ikac", blocks, columns, preferred_element_type=jnp.float32)
    near = jnp.where(live[:, :, None, None], near, 0.0).astype(jnp.bfloat16)
    terms = jnp.einsum("ibd,ikbc->ikdc", prolong, near, preferred_element_type=jnp.float32)
    terms = terms.reshape(shard_rows * slot_count, coarse_cols * coarse_cols)
    target = (agg[:, None] * CSLOT + rap_slot).reshape(-1)
    target_ids = jnp.arange(target_count, dtype=jnp.int32)
    placing = ((target_ids[:, None] == target[None, :]) & live.reshape(-1)[None, :]).astype(
        jnp.float32
    )
    total = jnp.dot(
        placing, terms, precision=lax.Precision.HIGHEST, preferred_element_type=jnp.float32
    )
    panel = total.reshape(panel_rows, CSLOT, coarse_cols * coarse_cols)
    return lax.psum_scatter(
        panel.astype(jnp.bfloat16), "grp", scatter_dimension=0, tiled=True
    ).astype(jnp.float32)


def solution(mesh):
    return jax.shard_map(
        on_device,
        mesh=mesh,
        in_specs=(
            P(("rows", "grp"), None, None),
            P(("rows", "grp"), None, None),
            P(("rows", "grp"), None),
            P(("rows", "grp"), None),
            P(("rows", "grp")),
            P(("rows", "grp"), None),
        ),
        out_specs=P(("rows", "grp"), None, None),
        check_vma=False,
    )
```

profile of v0, /device:TPU:6, one launch (start us, length us, event | category | flops | bytes accessed | tf_op | source)
XLA Modules:
  0.0 187.1 jit_solution(16907499097228794956)
XLA Ops:
  6.5 0.0 copy-start.2
  6.5 0.0 copy-start.1
  6.5 0.0 copy-start
  6.5 0.0 reduce-scatter.2.cloned.1.call-start
  6.5 0.8 broadcast_add_fusion.1
  7.3 5.1 %collective-permute-start = (s32[4]{0:T(128)S(1)}, s32[4]{0:T(128)S(1)}, u32[]{:S(2)}, u32[]{:S(2)}) collective-permute-start(s32[4]{0:T(128)S(1)} %get-tuple-element.5), channel_id=1, source_target_pairs={{8,0},{16,8},{24,16},{32,24},{40,32},{48,40},{56,48},{64,56},{72,6... | collective-permute-start | bytes 56 | tf_op jit(solution)/shard_map/ppermute | solution.py:13
  12.4 1.9 %collective-permute-start.2 = (s32[4]{0:T(128)S(1)}, s32[4]{0:T(128)S(1)}, u32[]{:S(2)}, u32[]{:S(2)}) collective-permute-start(s32[4]{0:T(128)S(1)} %get-tuple-element.6), channel_id=1, source_target_pairs={{0,8},{8,16},{16,24},{24,32},{32,40},{40,48},{48,56},{56,64},{64,7... | collective-permute-start | bytes 56 | tf_op jit(solution)/shard_map/ppermute | solution.py:13
  14.3 0.7 broadcast_maximum_fusion
  15.0 0.7 broadcast_compare_fusion
  15.7 0.1 copy.11
  15.8 0.1 reshape.58
  15.9 0.1 copy.9
  16.0 6.6 %copy.15 = bf16[48,64,512]{1,2,0:T(8,128)(2,1)} copy(bf16[48,64,512]{2,1,0:T(8,128)(2,1)} %param.6) | data formatting | bytes 6291456 | tf_op jit(solution)/shard_map/reshape | solution.py:34
  22.6 0.1 and.15
  22.7 0.0 copy-done.2
  22.7 0.0 copy-done.1
  22.7 0.1 copy.8
  22.8 0.1 eq.30
  22.9 0.0 collective-permute-done
  23.0 0.0 copy-done
  23.0 0.6 gather_fusion
  23.5 0.1 broadcast_select_fusion.1
  23.6 1.9 %collective-permute-start.1 = (bf16[4,64,128]{2,1,0:T(8,128)(2,1)S(1)}, bf16[4,64,128]{2,1,0:T(8,128)(2,1)S(1)}, u32[]{:S(2)}, u32[]{:S(2)}) collective-permute-start(bf16[4,64,128]{2,1,0:T(8,128)(2,1)S(1)} %broadcast_select_fusion.1), channel_id=1, source_target_pairs={{0,8},{8,16},{16,24},{24,32},{32,40},{40,48},{48,56},{56,64},{64,7... | collective-permute-start | bytes 196616 | tf_op jit(solution)/shard_map/ppermute | solution.py:13
  25.5 0.0 collective-permute-done.2
  25.6 0.6 gather_fusion.1
  26.2 0.1 broadcast_select_fusion
  26.2 5.7 %collective-permute-start.3 = (bf16[4,64,128]{2,1,0:T(8,128)(2,1)S(1)}, bf16[4,64,128]{2,1,0:T(8,128)(2,1)S(1)}, u32[]{:S(2)}, u32[]{:S(2)}) collective-permute-start(bf16[4,64,128]{2,1,0:T(8,128)(2,1)S(1)} %broadcast_select_fusion), channel_id=1, source_target_pairs={{8,0},{16,8},{24,16},{32,24},{40,32},{48,40},{56,48},{64,56},{72,6... | collective-permute-start | bytes 196616 | tf_op jit(solution)/shard_map/ppermute | solution.py:13
  32.0 0.0 collective-permute-done.1
  32.0 1.9 collective-permute-done.3
  33.9 0.1 pad_maximum_fusion
  34.0 13.3 %gather_fusion.2 = bf16[384,64,128]{2,1,0:T(8,128)(2,1)} fusion(bf16[56,64,128]{2,1,0:T(8,128)(2,1)S(1)} %pad_maximum_fusion, s32[1024]{0:T(1024)S(1)} %pad_clamp_fusion), kind=kCustom, calls=%fused_computation.2 | custom fusion | bytes 12584448 | tf_op jit(solution)/shard_map/gather | solution.py:33
  47.3 15.2 %convolution_bitcast_fusion = f32[48,8,128,128]{2,3,1,0:T(8,128)} fusion(pred[48,8]{1,0:T(8,128)(4,1)S(1)} %copy.9, bf16[48,8,64,128]{3,2,1,0:T(8,128)(2,1)} %bitcast.22, bf16[48,64,8,64]{1,3,2,0:T(8,128)(2,1)} %bitcast.21, bf16[48,64,128]{2,1,0:T(8,128)(2,1)S(1)} %copy-done), kind=kOutput, calls=%fused_computation.5 | convolution fusion | flops 1214251008 | bytes 35389824 | tf_op jit(solution)/shard_map/ibd,ikbc->ikdc/dot_general | solution.py:39
  62.5 24.6 %copy.12 = f32[48,8,128,128]{3,2,1,0:T(8,128)} copy(f32[48,8,128,128]{2,3,1,0:T(8,128)} %convolution_bitcast_fusion) | data formatting | bytes 50331648 | tf_op jit(solution)/shard_map/ibd,ikbc->ikdc/transpose | solution.py:39
  87.2 27.1 %reshape.69 = f32[384,16384,1]{1,0,2:T(8,128)} reshape(f32[48,8,128,128]{3,2,1,0:T(8,128)} %copy.12) | data formatting | bytes 50331648 | tf_op jit(solution)/shard_map/reshape | solution.py:40
  114.2 15.8 %convolution_convert_fusion = bf16[8,8,16384]{2,1,0:T(8,128)(2,1)} fusion(f32[384,16384,1]{1,0,2:T(8,128)} %reshape.69, s32[384]{0:T(512)S(1)} %eq.30, s32[8,8]{1,0:T(8,128)S(1)} %multiply_add_fusion, pred[384]{0:T(512)(128)(4,1)S(1)} %and.15), kind=kOutput, calls=%fused_computation.3 | convolution fusion | flops 4832935936 | bytes 27265152 | tf_op jit(solution)/shard_map/dot_general | solution.py:46
  130.0 0.0 reduce-scatter.2.cloned.1.call-update
  130.0 48.4 %reduce-scatter.2.cloned.1.call-done = bf16[1,8,16384]{2,1,0:T(8,128)(2,1)} async-done(((bf16[8,8,16384]{2,1,0:T(8,128)(2,1)}), bf16[1,8,16384]{2,1,0:T(8,128)(2,1)}) %reduce-scatter.2.cloned.1.call-update) | async-done | bytes 262160 | tf_op jit(solution)/shard_map/reduce_scatter | solution.py:50
  178.5 1.8 convert_element_type.19
  (11 shorter events, 0.1 us)
Async XLA Ops:
  6.5 16.2 %copy-start.2 = (s32[48]{0:T(128)S(1)}, s32[48]{0:T(128)}, u32[]{:S(2)}) copy-start(s32[48]{0:T(128)} %param.10) | copy-start | bytes 580
  6.5 16.2 %copy-start.1 = (s32[48,8]{0,1:T(8,128)S(1)}, s32[48,8]{0,1:T(8,128)}, u32[]{:S(2)}) copy-start(s32[48,8]{0,1:T(8,128)} %param.11) | copy-start | bytes 4612
  6.5 16.4 %copy-start = (bf16[48,64,128]{2,1,0:T(8,128)(2,1)S(1)}, bf16[48,64,128]{2,1,0:T(8,128)(2,1)}, u32[]{:S(2)}) copy-start(bf16[48,64,128]{2,1,0:T(8,128)(2,1)} %param.7) | copy-start | bytes 2359300
  6.5 171.9 %reduce-scatter.2.cloned.1.call-start = ((), (), s32[]{:S(2)}) async-start(), calls=%async_computation.1 | async-start | bytes 2359296 | tf_op jit(solution)/shard_map/reduce_scatter | solution.py:50
  7.3 15.6 %collective-permute-start = (s32[4]{0:T(128)S(1)}, s32[4]{0:T(128)S(1)}, u32[]{:S(2)}, u32[]{:S(2)}) collective-permute-start(s32[4]{0:T(128)S(1)} %get-tuple-element.5), channel_id=1, source_target_pairs={{8,0},{16,8},{24,16},{32,24},{40,32},{48,40},{56,48},{64,56},{72,6... | collective-permute-start | bytes 56 | tf_op jit(solution)/shard_map/ppermute | solution.py:13
  12.4 13.2 %collective-permute-start.2 = (s32[4]{0:T(128)S(1)}, s32[4]{0:T(128)S(1)}, u32[]{:S(2)}, u32[]{:S(2)}) collective-permute-start(s32[4]{0:T(128)S(1)} %get-tuple-element.6), channel_id=1, source_target_pairs={{0,8},{8,16},{16,24},{24,32},{32,40},{40,48},{48,56},{56,64},{64,7... | collective-permute-start | bytes 56 | tf_op jit(solution)/shard_map/ppermute | solution.py:13
  23.6 8.4 %collective-permute-start.1 = (bf16[4,64,128]{2,1,0:T(8,128)(2,1)S(1)}, bf16[4,64,128]{2,1,0:T(8,128)(2,1)S(1)}, u32[]{:S(2)}, u32[]{:S(2)}) collective-permute-start(bf16[4,64,128]{2,1,0:T(8,128)(2,1)S(1)} %broadcast_select_fusion.1), channel_id=1, source_target_pairs={{0,8},{8,16},{16,24},{24,32},{32,40},{40,48},{48,56},{56,64},{64,7... | collective-permute-start | bytes 196616 | tf_op jit(solution)/shard_map/ppermute | solution.py:13
  26.2 7.6 %collective-permute-start.3 = (bf16[4,64,128]{2,1,0:T(8,128)(2,1)S(1)}, bf16[4,64,128]{2,1,0:T(8,128)(2,1)S(1)}, u32[]{:S(2)}, u32[]{:S(2)}) collective-permute-start(bf16[4,64,128]{2,1,0:T(8,128)(2,1)S(1)} %broadcast_select_fusion), channel_id=1, source_target_pairs={{8,0},{16,8},{24,16},{32,24},{40,32},{48,40},{56,48},{64,56},{72,6... | collective-permute-start | bytes 196616 | tf_op jit(solution)/shard_map/ppermute | solution.py:13
Sparse Core Ops, SparseCore 0:
  130.1 48.2 reduce-scatter.1
where the time goes:
time: 188 us; the launch traced here: 187 us
  local copies, waits for them, and re-layouts  73.3 us (39%)
  waiting for transfers between devices  50.3 us (27%)
  matrix products  31 us (16%)
  starting transfers between devices  14.6 us (8%)
  between operations  13.6 us (7%)
  other arithmetic  4.24 us (2%)
    reduce_scatter x1, waiting for transfers between devices, on_device(): lax.psum_scatter(panel.astype(jnp.bfloat16), 'grp', scatter_dimension=0,...  48.4 us
    reshape x1, local copies, waits for them, and re-layouts, on_device(): terms = terms.reshape(shard_rows * slot_count, coarse_cols * coarse_cols)  27.1 us
    transpose x1, local copies, waits for them, and re-layouts, on_device(): jnp.einsum('ibd,ikbc->ikdc', prolong, near, preferred_element_type=jnp.fl...  24.6 us
    dot_general x1, matrix products, on_device(): jnp.dot(placing, terms, precision=lax.Precision.HIGHEST, preferred_elemen...  15.8 us
    dot_general x1, matrix products, on_device(): jnp.einsum('ibd,ikbc->ikdc', prolong, near, preferred_element_type=jnp.fl...  15.2 us
    ppermute x4, starting transfers between devices, from_behind(): lax.ppermute(value, axis, [(source, source + steps) for source in range(f...  14.6 us
    gather x1, local copies, waits for them, and re-layouts, on_device(): columns = buffer[jnp.maximum(a_cols, 0)]  13.3 us
    reshape x1, local copies, waits for them, and re-layouts, on_device(): blocks = a_blocks.reshape(shard_rows, block_cells, slot_count, block_cells)  6.64 us
  transfers between devices with their start and end apart: 5, of which 2 were waited for; matrix products, arithmetic and copies ran while one was open for 5% of the time, Pallas kernels for 0%

commit v1 on v0

v1 whole, which is shorter than its diff:
```python
import functools

import jax
import jax.numpy as jnp
from jax import lax
from jax.experimental import pallas as pl
from jax.experimental.pallas import tpu as pltpu
from jax.sharding import PartitionSpec as P

CSLOT = 8
MESH = pl.DeviceIdType.MESH


def lane_pair(left, right, rows):
    lanes = lax.broadcasted_iota(jnp.int32, (rows, 128), 1)
    return jnp.where(lanes < 64, left, right)


def indicator(value, wanted):
    return jnp.where(value == wanted, 1.0, 0.0).astype(jnp.bfloat16)


def kernel(
    row_count, grp_count,
    reads_ref, cols_ref, agg_ref, rap_ref, a_hbm, p_hbm,
    out_ref,
    a_v, p_loc, p_all, p_masked, spread, near, req_v, req_s, stage, outgoing, incoming,
    local_sem, req_send, req_recv, rep_send, rep_recv, ring_send, ring_recv,
):
    shard_rows, cells, _ = a_v.shape
    slot_count = cols_ref.shape[0]
    cap = stage.shape[1]
    half = grp_count // 2
    row, grp = lax.axis_index("rows"), lax.axis_index("grp")
    above, below = lax.rem(row + 1, row_count), lax.rem(row + row_count - 1, row_count)
    ahead, behind = lax.rem(grp + 1, grp_count), lax.rem(grp + grp_count - 1, grp_count)

    a_copy = pltpu.make_async_copy(a_hbm, a_v, local_sem.at[0])
    p_copy = pltpu.make_async_copy(p_hbm, p_loc, local_sem.at[1])
    all_copy = pltpu.make_async_copy(p_hbm, p_all.at[pl.ds(0, shard_rows)], local_sem.at[2])
    p_copy.start()
    a_copy.start()
    all_copy.start()

    barrier = pltpu.get_barrier_semaphore()
    for device in ({"rows": above}, {"rows": below}, {"grp": ahead}, {"grp": behind}):
        pl.semaphore_signal(barrier, inc=1, device_id=device, device_id_type=MESH)
    pl.semaphore_wait(barrier, 4)

    def request(side):
        return pltpu.make_async_remote_copy(
            src_ref=reads_ref,
            dst_ref=req_v.at[1 - side],
            send_sem=req_send.at[side],
            recv_sem=req_recv.at[1 - side],
            device_id={"rows": (below, above)[side]},
            device_id_type=MESH,
        )

    def reply(side):
        return pltpu.make_async_remote_copy(
            src_ref=stage.at[side],
            dst_ref=p_all.at[pl.ds(shard_rows + (1 - side) * cap, cap)],
            send_sem=rep_send.at[side],
            recv_sem=rep_recv.at[1 - side],
            device_id={"rows": (below, above)[side]},
            device_id_type=MESH,
        )

    for side in (0, 1):
        request(side).start()

    p_copy.wait()

    @pl.loop(0, shard_rows // 2)
    def _(pair):
        block = p_loc[pl.ds(pair * 2, 2)].reshape(128, 128).T
        owner = lane_pair(agg_ref[pair * 2], agg_ref[pair * 2 + 1], 16)
        lanes = pl.ds(pl.multiple_of(pair * 128, 128), 128)
        for q in range(grp_count):
            keep = indicator(owner, q)
            p_masked[q, :, lanes] = block * jnp.concatenate([keep] * 8, axis=0)

    for side in (0, 1):
        request(side).wait()
    req_copy = pltpu.make_async_copy(req_v, req_s, local_sem.at[3])
    req_copy.start()
    req_copy.wait()
    for side in (0, 1):
        for c in range(cap):
            stage[side, c] = p_loc[jnp.maximum(req_s[side, 1 - side, c], 0)]
        reply(side).start()

    a_copy.wait()

    @pl.loop(0, shard_rows)
    def _(i):
        places = [
            jnp.where(cols_ref[k, i] >= 0, rap_ref[k, i], -1) for k in range(slot_count)
        ]
        for k in range(0, slot_count, 2):
            lanes = pl.ds(k * cells, 2 * cells)
            block = a_v[i, :, lanes]
            place = lane_pair(places[k], places[k + 1], 16)
            for s in range(CSLOT):
                keep = indicator(place, s)
                spread[i, pl.ds(s * cells, cells), lanes] = block * jnp.concatenate(
                    [keep] * (cells // 16), axis=0
                )

    all_copy.wait()
    for side in (0, 1):
        reply(side).wait()

    @pl.loop(0, shard_rows)
    def _(i):
        columns = jnp.concatenate(
            [p_all[jnp.maximum(cols_ref[k, i], 0)] for k in range(slot_count)], axis=0
        )
        product = jnp.dot(spread[i], columns, preferred_element_type=jnp.float32)
        product = product.astype(jnp.bfloat16)
        rows = pl.ds(pl.multiple_of(i * cells, cells), cells)
        for s in range(CSLOT):
            near[s // 2, rows, (s % 2) * 128 : (s % 2 + 1) * 128] = product[
                s * cells : (s + 1) * cells
            ]

    def hop(way, step, s):
        return pltpu.make_async_remote_copy(
            src_ref=outgoing.at[way, step, s],
            dst_ref=incoming.at[way, step, s],
            send_sem=ring_send.at[way, step, s],
            recv_sem=ring_recv.at[way, step, s],
            device_id={"grp": (ahead, behind)[way]},
            device_id_type=MESH,
        )

    def own_terms(q, pair):
        return jnp.dot(p_masked[q], near[pair], preferred_element_type=jnp.float32)

    def forward(way, step, pair, receives):
        away = half - step
        q = lax.rem(grp + (away if way == 0 else grp_count - away), grp_count)
        terms = own_terms(q, pair)
        for h in (0, 1):
            s = pair * 2 + h
            total = terms[:, h * 128 : (h + 1) * 128]
            if receives:
                hop(way, step - 1, s).wait_recv()
                total = total + incoming[way, step - 1, s].astype(jnp.float32)
            outgoing[way, step, s] = total.astype(jnp.bfloat16)
            hop(way, step, s).start()

    @pl.loop(0, 2)
    def _(j):
        forward(0, 0, j, False)
        forward(1, 0, j + 2, False)

    @pl.loop(0, 2)
    def _(j):
        forward(0, 1, j + 2, False)
        forward(1, 1, j, False)

    @pl.loop(2, 4 * (half - 1))
    def _(n):
        step, j = 1 + n // 4, n % 4
        forward(0, step, (j + 2) % 4, True)
        forward(1, step, j, True)

    @pl.loop(0, 4)
    def _(pair):
        terms = own_terms(grp, pair)
        for h in (0, 1):
            s = pair * 2 + h
            total = terms[:, h * 128 : (h + 1) * 128]
            for way in (0, 1):
                hop(way, half - 1, s).wait_recv()
                total = total + incoming[way, half - 1, s].astype(jnp.float32)
            out_ref[s] = total

    for way in (0, 1):
        @pl.loop(0, 4)
        def _(s, way=way):
            hop(way, 0, s + 4 * way).wait_send()

        @pl.loop(8, 8 * half)
        def _(n, way=way):
            hop(way, n // 8, n % 8).wait_send()


def on_device(row_count, grp_count, a_blocks, prolong, a_cols, read_slots, agg, rap_slot):
    shard_rows, cells, width = a_blocks.shape
    coarse = prolong.shape[2]
    cap = read_slots.shape[1]
    half = grp_count // 2
    vmem = pl.BlockSpec(memory_space=pltpu.VMEM)
    smem = pl.BlockSpec(memory_space=pltpu.SMEM)
    hbm = pl.BlockSpec(memory_space=pl.ANY)
    b16 = jnp.bfloat16
    dma = pltpu.SemaphoreType.DMA
    out = pl.pallas_call(
        functools.partial(kernel, row_count, grp_count),
        out_shape=jax.ShapeDtypeStruct((CSLOT, coarse, coarse), jnp.float32),
        in_specs=[vmem, smem, smem, smem, hbm, hbm],
        out_specs=vmem,
        scratch_shapes=[
            pltpu.VMEM((shard_rows, cells, width), b16),
            pltpu.VMEM((shard_rows, cells, coarse), b16),
            pltpu.VMEM((shard_rows + 2 * cap, cells, coarse), b16),
            pltpu.VMEM((grp_count, coarse, shard_rows * cells), b16),
            pltpu.VMEM((shard_rows, CSLOT * cells, width), b16),
            pltpu.VMEM((CSLOT // 2, shard_rows * cells, 2 * coarse), b16),
            pltpu.VMEM((2, 2, cap), jnp.int32),
            pltpu.SMEM((2, 2, cap), jnp.int32),
            pltpu.VMEM((2, cap, cells, coarse), b16),
            pltpu.VMEM((2, half, CSLOT, coarse, coarse), b16),
            pltpu.VMEM((2, half, CSLOT, coarse, coarse), b16),
            dma((4,)),
            dma((2,)),
            dma((2,)),
            dma((2,)),
            dma((2,)),
            dma((2, half, CSLOT)),
            dma((2, half, CSLOT)),
        ],
        compiler_params=pltpu.CompilerParams(
            collective_id=0, has_side_effects=True, vmem_limit_bytes=58 * 1024 * 1024
        ),
    )(read_slots, a_cols.T, agg, rap_slot.T, a_blocks, prolong)
    return out.reshape(1, CSLOT, coarse * coarse)


def solution(mesh):
    return jax.shard_map(
        functools.partial(on_device, mesh.shape["rows"], mesh.shape["grp"]),
        mesh=mesh,
        in_specs=(
            P(("rows", "grp"), None, None),
            P(("rows", "grp"), None, None),
            P(("rows", "grp"), None),
            P(("rows", "grp"), None),
            P(("rows", "grp")),
            P(("rows", "grp"), None),
        ),
        out_specs=P(("rows", "grp"), None, None),
        check_vma=False,
    )
```

time: 188 us -> 62.7 us (0.33)
  the two profiles are of different devices: /device:TPU:6 before, /device:TPU:1 now
where the time goes in v1:
time: 62.7 us; the launch traced here: 62.5 us
  Pallas kernels  60.5 us (96%)
  local copies, waits for them, and re-layouts  1.93 us (3%)
    pallas_call x1, Pallas kernels, on_device(): pl.pallas_call(functools.partial(kernel, row_count, grp_count), out_shape...  60.5 us
    reshape x1, local copies, waits for them, and re-layouts, on_device(): return out.reshape(1, CSLOT, coarse * coarse)  1.93 us

profile of v1, /device:TPU:1, one launch (start us, length us, event | category | flops | bytes accessed | tf_op | source)
XLA Modules:
  0.0 62.5 jit_solution(12183354630985078517)
XLA Ops:
  0.0 60.5 %shard_map.64 = f32[8,128,128]{2,1,0:T(8,128)} custom-call(s32[2,4]{1,0:T(2,128)} %reads_ref.1, s32[8,48]{1,0:T(8,128)} %bitcast.2, s32[48]{0:T(128)} %agg_ref.1, s32[8,48]{1,0:T(8,128)} %bitcast.3, bf16[48,64,512]{2,1,0:T(8,128)(2,1)} %a_hbm.1, bf16[48,64,128]{2,1,0:T(8,128)(2,1)} %p_hbm.1), custom_call_target="tpu_custom_call" | custom-call | tf_op jit(solution)/shard_map/pallas_call | solution.py:201
  60.5 1.9 %reshape.3 = f32[1,8,16384]{2,1,0:T(8,128)} reshape(f32[8,128,128]{2,1,0:T(8,128)} %shard_map.64) | data formatting | bytes 1048576 | tf_op jit(solution)/shard_map/reshape | solution.py:230

commit v2 on v1

--- a/solution.py
+++ b/solution.py
@@ -24,7 +24,7 @@
     row_count, grp_count,
     reads_ref, cols_ref, agg_ref, rap_ref, a_hbm, p_hbm,
     out_ref,
-    a_v, p_loc, p_all, p_masked, spread, near, req_v, req_s, stage, outgoing, incoming,
+    a_v, p_loc, p_all, p_turned, p_masked, near, total_v, req_v, req_s, stage, outgoing, incoming,
     local_sem, req_send, req_recv, rep_send, rep_recv, ring_send, ring_recv,
 ):
     shard_rows, cells, _ = a_v.shape
@@ -72,14 +72,10 @@
 
     p_copy.wait()
 
-    @pl.loop(0, shard_rows // 2)
+    @pl.loop(0, shard_rows // 2, unroll=4)
     def _(pair):
-        block = p_loc[pl.ds(pair * 2, 2)].reshape(128, 128).T
-        owner = lane_pair(agg_ref[pair * 2], agg_ref[pair * 2 + 1], 16)
         lanes = pl.ds(pl.multiple_of(pair * 128, 128), 128)
-        for q in range(grp_count):
-            keep = indicator(owner, q)
-            p_masked[q, :, lanes] = block * jnp.concatenate([keep] * 8, axis=0)
+        p_turned[:, lanes] = p_loc[pl.ds(pair * 2, 2)].reshape(128, 128).T
 
     for side in (0, 1):
         request(side).wait()
@@ -91,34 +87,42 @@
             stage[side, c] = p_loc[jnp.maximum(req_s[side, 1 - side, c], 0)]
         reply(side).start()
 
+    @pl.loop(0, shard_rows // 2)
+    def _(pair):
+        lanes = pl.ds(pl.multiple_of(pair * 128, 128), 128)
+        block = p_turned[:, lanes]
+        owner = lane_pair(agg_ref[pair * 2], agg_ref[pair * 2 + 1], 16)
+        for q in range(grp_count):
+            keep = indicator(owner, q)
+            p_masked[q, :, lanes] = block * jnp.concatenate([keep] * 8, axis=0)
+
     a_copy.wait()
-
-    @pl.loop(0, shard_rows)
+    all_copy.wait()
+    for side in (0, 1):
+        reply(side).wait()
+
+    @pl.loop(0, shard_rows, unroll=4)
     def _(i):
+        columns = jnp.concatenate(
+            [p_all[jnp.maximum(cols_ref[k, i], 0)] for k in range(slot_count)], axis=0
+        )
         places = [
             jnp.where(cols_ref[k, i] >= 0, rap_ref[k, i], -1) for k in range(slot_count)
         ]
+        spread = []
         for k in range(0, slot_count, 2):
-            lanes = pl.ds(k * cells, 2 * cells)
-            block = a_v[i, :, lanes]
+            block = a_v[i, :, k * cells : (k + 2) * cells]
             place = lane_pair(places[k], places[k + 1], 16)
-            for s in range(CSLOT):
-                keep = indicator(place, s)
-                spread[i, pl.ds(s * cells, cells), lanes] = block * jnp.concatenate(
-                    [keep] * (cells // 16), axis=0
+            keeps = [indicator(place, s) for s in range(CSLOT)]
+            spread.append(
+                jnp.concatenate(
+                    [block * jnp.concatenate([keep] * (cells // 16), axis=0) for keep in keeps],
+                    axis=0,
                 )
-
-    all_copy.wait()
-    for side in (0, 1):
-        reply(side).wait()
-
-    @pl.loop(0, shard_rows)
-    def _(i):
-        columns = jnp.concatenate(
-            [p_all[jnp.maximum(cols_ref[k, i], 0)] for k in range(slot_count)], axis=0
-        )
-        product = jnp.dot(spread[i], columns, preferred_element_type=jnp.float32)
-        product = product.astype(jnp.bfloat16)
+            )
+        product = jnp.dot(
+            jnp.concatenate(spread, axis=1), columns, preferred_element_type=jnp.float32
+        ).astype(jnp.bfloat16)
         rows = pl.ds(pl.multiple_of(i * cells, cells), cells)
         for s in range(CSLOT):
             near[s // 2, rows, (s % 2) * 128 : (s % 2 + 1) * 128] = product[
@@ -135,57 +139,77 @@
             device_id_type=MESH,
         )
 
-    def own_terms(q, pair):
-        return jnp.dot(p_masked[q], near[pair], preferred_element_type=jnp.float32)
-
-    def forward(way, step, pair, receives):
-        away = half - step
-        q = lax.rem(grp + (away if way == 0 else grp_count - away), grp_count)
-        terms = own_terms(q, pair)
+    def own_terms(first, second, pair):
+        left = jnp.concatenate([p_masked[first], p_masked[second]], axis=0)
+        return jnp.dot(left, near[pair], preferred_element_type=jnp.float32)
+
+    def forward(way, step, pair, terms, receives):
         for h in (0, 1):
             s = pair * 2 + h
-            total = terms[:, h * 128 : (h + 1) * 128]
+            total = terms[way * 128 : (way + 1) * 128, h * 128 : (h + 1) * 128]
             if receives:
                 hop(way, step - 1, s).wait_recv()
                 total = total + incoming[way, step - 1, s].astype(jnp.float32)
             outgoing[way, step, s] = total.astype(jnp.bfloat16)
             hop(way, step, s).start()
 
+    def both(step, pair):
+        away = half - step
+        return own_terms(
+            lax.rem(grp + away, grp_count), lax.rem(grp + grp_count - away, grp_count), pair
+        )
+
     @pl.loop(0, 2)
     def _(j):
-        forward(0, 0, j, False)
-        forward(1, 0, j + 2, False)
+        for pair, way in ((j, 0), (j + 2, 1)):
+            terms = own_terms(lax.rem(grp + half, grp_count), grp, pair)
+            for h in (0, 1):
+                s = pair * 2 + h
+                lanes = slice(h * 128, (h + 1) * 128)
+                outgoing[way, 0, s] = terms[:128, lanes].astype(jnp.bfloat16)
+                hop(way, 0, s).start()
+                total_v[pl.ds(pl.multiple_of(s * 128, 128), 128)] = terms[128:, lanes]
 
     @pl.loop(0, 2)
     def _(j):
-        forward(0, 1, j + 2, False)
-        forward(1, 1, j, False)
-
-    @pl.loop(2, 4 * (half - 1))
+        for pair, fresh in ((j, 1), (j + 2, 0)):
+            terms = both(1, pair)
+            forward(fresh, 1, pair, terms, False)
+            forward(1 - fresh, 1, pair, terms, True)
+
+    @pl.loop(0, 4 * (half - 2))
     def _(n):
-        step, j = 1 + n // 4, n % 4
-        forward(0, step, (j + 2) % 4, True)
-        forward(1, step, j, True)
-
-    @pl.loop(0, 4)
-    def _(pair):
-        terms = own_terms(grp, pair)
-        for h in (0, 1):
-            s = pair * 2 + h
-            total = terms[:, h * 128 : (h + 1) * 128]
-            for way in (0, 1):
-                hop(way, half - 1, s).wait_recv()
-                total = total + incoming[way, half - 1, s].astype(jnp.float32)
-            out_ref[s] = total
+        step, pair = 2 + n // 4, (n % 4) // 2 + 2 * (n % 2)
+        terms = both(step, pair)
+        forward(0, step, pair, terms, True)
+        forward(1, step, pair, terms, True)
 
     for way in (0, 1):
         @pl.loop(0, 4)
         def _(s, way=way):
             hop(way, 0, s + 4 * way).wait_send()
 
-        @pl.loop(8, 8 * half)
+        @pl.loop(8, 8 * (half - 1))
         def _(n, way=way):
             hop(way, n // 8, n % 8).wait_send()
+
+    @pl.loop(0, 8)
+    def _(n):
+        s = 4 * ((n // 2) % 2) + 2 * (n // 4) + n % 2
+        rows = pl.ds(pl.multiple_of(s * 128, 128), 128)
+        total = total_v[rows]
+        for way in (0, 1):
+            hop(way, half - 1, s).wait_recv()
+            total = total + incoming[way, half - 1, s].astype(jnp.float32)
+        total_v[rows] = total
+
+    for d in range(128):
+        out_ref[0, :, d * 128 : (d + 1) * 128] = total_v[pl.ds(d, CSLOT, stride=128)]
+
+    for way in (0, 1):
+        @pl.loop(0, 8)
+        def _(s, way=way):
+            hop(way, half - 1, s).wait_send()
 
 
 def on_device(row_count, grp_count, a_blocks, prolong, a_cols, read_slots, agg, rap_slot):
@@ -198,18 +222,19 @@
     hbm = pl.BlockSpec(memory_space=pl.ANY)
     b16 = jnp.bfloat16
     dma = pltpu.SemaphoreType.DMA
-    out = pl.pallas_call(
+    return pl.pallas_call(
         functools.partial(kernel, row_count, grp_count),
-        out_shape=jax.ShapeDtypeStruct((CSLOT, coarse, coarse), jnp.float32),
+        out_shape=jax.ShapeDtypeStruct((1, CSLOT, coarse * coarse), jnp.float32),
         in_specs=[vmem, smem, smem, smem, hbm, hbm],
         out_specs=vmem,
         scratch_shapes=[
             pltpu.VMEM((shard_rows, cells, width), b16),
             pltpu.VMEM((shard_rows, cells, coarse), b16),
             pltpu.VMEM((shard_rows + 2 * cap, cells, coarse), b16),
+            pltpu.VMEM((coarse, shard_rows * cells), b16),
             pltpu.VMEM((grp_count, coarse, shard_rows * cells), b16),
-            pltpu.VMEM((shard_rows, CSLOT * cells, width), b16),
             pltpu.VMEM((CSLOT // 2, shard_rows * cells, 2 * coarse), b16),
+            pltpu.VMEM((CSLOT * coarse, coarse), jnp.float32),
             pltpu.VMEM((2, 2, cap), jnp.int32),
             pltpu.SMEM((2, 2, cap), jnp.int32),
             pltpu.VMEM((2, cap, cells, coarse), b16),
@@ -224,10 +249,9 @@
             dma((2, half, CSLOT)),
         ],
         compiler_params=pltpu.CompilerParams(
-            collective_id=0, has_side_effects=True, vmem_limit_bytes=58 * 1024 * 1024
+            collective_id=0, has_side_effects=True, vmem_limit_bytes=56 * 1024 * 1024
         ),
     )(read_slots, a_cols.T, agg, rap_slot.T, a_blocks, prolong)
-    return out.reshape(1, CSLOT, coarse * coarse)
 
 
 def solution(mesh):

time: 62.7 us -> 56.5 us (0.901)
  the two profiles are of different devices: /device:TPU:1 before, /device:TPU:64 now
where the time goes in v2:
time: 56.5 us; the launch traced here: 56.3 us
  Pallas kernels  54.4 us (96%)
  local copies, waits for them, and re-layouts  1.87 us (3%)
    pallas_call x1, Pallas kernels, on_device(): pl.pallas_call(functools.partial(kernel, row_count, grp_count), out_shape...  54.4 us
    unnamed x1, local copies, waits for them, and re-layouts  1.87 us

profile of v2, /device:TPU:64, one launch (start us, length us, event | category | flops | bytes accessed | tf_op | source)
XLA Modules:
  0.0 56.3 jit_solution(9107110292341022253)
XLA Ops:
  0.0 54.4 %shard_map.64 = f32[1,8,16384]{2,1,0:T(8,128)} custom-call(s32[2,4]{1,0:T(2,128)} %reads_ref.1, s32[8,48]{1,0:T(8,128)} %bitcast.2, s32[48]{0:T(128)} %agg_ref.1, s32[8,48]{1,0:T(8,128)} %bitcast.3, bf16[48,64,512]{2,1,0:T(8,128)(2,1)} %a_hbm.1, bf16[48,64,128]{2,1,0:T(8,128)(2,1)} %p_hbm.1), custom_call_target="tpu_custom_call" | custom-call | tf_op jit(solution)/shard_map/pallas_call | solution.py:225
  54.5 1.9 %copy.8 = f32[1,8,16384]{2,1,0:T(8,128)} copy(f32[1,8,16384]{2,1,0:T(8,128)} %shard_map.64) | data formatting | bytes 1048576

commit v3 on v2

--- a/solution.py
+++ b/solution.py
@@ -22,8 +22,9 @@
 
 def kernel(
     row_count, grp_count,
-    reads_ref, cols_ref, agg_ref, rap_ref, a_hbm, p_hbm,
+    reads_hbm, cols_hbm, agg_hbm, rap_hbm, a_hbm, p_hbm,
     out_ref,
+    cols_ref, agg_ref, rap_ref,
     a_v, p_loc, p_all, p_turned, p_masked, near, total_v, req_v, req_s, stage, outgoing, incoming,
     local_sem, req_send, req_recv, rep_send, rep_recv, ring_send, ring_recv,
 ):
@@ -41,6 +42,14 @@
     p_copy.start()
     a_copy.start()
     all_copy.start()
+    index_copies = [
+        pltpu.make_async_copy(source, target, local_sem.at[4 + n])
+        for n, (source, target) in enumerate(
+            ((agg_hbm, agg_ref), (cols_hbm, cols_ref), (rap_hbm, rap_ref))
+        )
+    ]
+    for copy in index_copies:
+        copy.start()
 
     barrier = pltpu.get_barrier_semaphore()
     for device in ({"rows": above}, {"rows": below}, {"grp": ahead}, {"grp": behind}):
@@ -49,7 +58,7 @@
 
     def request(side):
         return pltpu.make_async_remote_copy(
-            src_ref=reads_ref,
+            src_ref=reads_hbm,
             dst_ref=req_v.at[1 - side],
             send_sem=req_send.at[side],
             recv_sem=req_recv.at[1 - side],
@@ -87,6 +96,9 @@
             stage[side, c] = p_loc[jnp.maximum(req_s[side, 1 - side, c], 0)]
         reply(side).start()
 
+    for copy in index_copies:
+        copy.wait()
+
     @pl.loop(0, shard_rows // 2)
     def _(pair):
         lanes = pl.ds(pl.multiple_of(pair * 128, 128), 128)
@@ -101,8 +113,7 @@
     for side in (0, 1):
         reply(side).wait()
 
-    @pl.loop(0, shard_rows, unroll=4)
-    def _(i):
+    def slot_sums(i, slots):
         columns = jnp.concatenate(
             [p_all[jnp.maximum(cols_ref[k, i], 0)] for k in range(slot_count)], axis=0
         )
@@ -113,7 +124,7 @@
         for k in range(0, slot_count, 2):
             block = a_v[i, :, k * cells : (k + 2) * cells]
             place = lane_pair(places[k], places[k + 1], 16)
-            keeps = [indicator(place, s) for s in range(CSLOT)]
+            keeps = [indicator(place, s) for s in slots]
             spread.append(
                 jnp.concatenate(
                     [block * jnp.concatenate([keep] * (cells // 16), axis=0) for keep in keeps],
@@ -124,10 +135,23 @@
             jnp.concatenate(spread, axis=1), columns, preferred_element_type=jnp.float32
         ).astype(jnp.bfloat16)
         rows = pl.ds(pl.multiple_of(i * cells, cells), cells)
-        for s in range(CSLOT):
+        for n, s in enumerate(slots):
             near[s // 2, rows, (s % 2) * 128 : (s % 2 + 1) * 128] = product[
-                s * cells : (s + 1) * cells
+                n * cells : (n + 1) * cells
             ]
+
+    first_half, second_half = range(CSLOT // 2), range(CSLOT // 2, CSLOT)
+
+    @pl.loop(0, shard_rows, unroll=4)
+    def _(i):
+        slot_sums(i, first_half)
+
+    batch = shard_rows // 6
+
+    def later_sums(n):
+        @pl.loop(0, batch, unroll=min(4, batch))
+        def _(j):
+            slot_sums(n * batch + j, second_half)
 
     def hop(way, step, s):
         return pltpu.make_async_remote_copy(
@@ -146,70 +170,82 @@
     def forward(way, step, pair, terms, receives):
         for h in (0, 1):
             s = pair * 2 + h
-            total = terms[way * 128 : (way + 1) * 128, h * 128 : (h + 1) * 128]
+            total = terms[:, h * 128 : (h + 1) * 128]
             if receives:
                 hop(way, step - 1, s).wait_recv()
                 total = total + incoming[way, step - 1, s].astype(jnp.float32)
             outgoing[way, step, s] = total.astype(jnp.bfloat16)
             hop(way, step, s).start()
 
-    def both(step, pair):
-        away = half - step
-        return own_terms(
-            lax.rem(grp + away, grp_count), lax.rem(grp + grp_count - away, grp_count), pair
-        )
+    def advance(long_way, step, pair):
+        forth, back = half - step, grp_count - (half - 1 - step)
+        if long_way == 1:
+            forth, back = grp_count - forth, grp_count - back
+        last = isinstance(step, int) and step == half - 1
+        terms = own_terms(lax.rem(grp + forth, grp_count), lax.rem(grp + back, grp_count), pair)
+        receives = not (isinstance(step, int) and step == 0)
+        forward(long_way, step, pair, terms[:128], receives)
+        if last:
+            for h in (0, 1):
+                rows = pl.ds(pl.multiple_of((pair * 2 + h) * 128, 128), 128)
+                total_v[rows] = terms[128:, h * 128 : (h + 1) * 128]
+        else:
+            forward(1 - long_way, step, pair, terms[128:], receives)
 
     @pl.loop(0, 2)
-    def _(j):
-        for pair, way in ((j, 0), (j + 2, 1)):
-            terms = own_terms(lax.rem(grp + half, grp_count), grp, pair)
-            for h in (0, 1):
-                s = pair * 2 + h
-                lanes = slice(h * 128, (h + 1) * 128)
-                outgoing[way, 0, s] = terms[:128, lanes].astype(jnp.bfloat16)
-                hop(way, 0, s).start()
-                total_v[pl.ds(pl.multiple_of(s * 128, 128), 128)] = terms[128:, lanes]
+    def _(n):
+        advance(0, 0, n)
+        later_sums(n)
+
+    @pl.loop(0, 2 * (half - 2))
+    def _(n):
+        advance(0, 1 + n // 2, n % 2)
+        if half > 2:
+            later_sums(2 + n)
+
+    for n in range(2 + 2 * (half - 2), 6):
+        later_sums(n)
+
+    @pl.loop(2, 4)
+    def _(pair):
+        advance(1, 0, pair)
 
     @pl.loop(0, 2)
-    def _(j):
-        for pair, fresh in ((j, 1), (j + 2, 0)):
-            terms = both(1, pair)
-            forward(fresh, 1, pair, terms, False)
-            forward(1 - fresh, 1, pair, terms, True)
-
-    @pl.loop(0, 4 * (half - 2))
+    def _(pair):
+        advance(0, half - 1, pair)
+
+    @pl.loop(0, 2 * (half - 2))
     def _(n):
-        step, pair = 2 + n // 4, (n % 4) // 2 + 2 * (n % 2)
-        terms = both(step, pair)
-        forward(0, step, pair, terms, True)
-        forward(1, step, pair, terms, True)
-
-    for way in (0, 1):
-        @pl.loop(0, 4)
-        def _(s, way=way):
-            hop(way, 0, s + 4 * way).wait_send()
-
-        @pl.loop(8, 8 * (half - 1))
-        def _(n, way=way):
-            hop(way, n // 8, n % 8).wait_send()
-
-    @pl.loop(0, 8)
-    def _(n):
-        s = 4 * ((n // 2) % 2) + 2 * (n // 4) + n % 2
+        advance(1, 1 + n // 2, 2 + n % 2)
+
+    @pl.loop(2, 4)
+    def _(pair):
+        advance(1, half - 1, pair)
+
+    def settle(way, long):
+        @pl.loop(0, 4 * (half if long else half - 1))
+        def _(n):
+            hop(way, n // 4, n % 4 + (4 if (way == 1) == long else 0)).wait_send()
+
+    settle(0, True)
+    settle(0, False)
+    settle(1, False)
+
+    @pl.loop(0, CSLOT)
+    def _(s):
         rows = pl.ds(pl.multiple_of(s * 128, 128), 128)
         total = total_v[rows]
+        early = s // 4
         for way in (0, 1):
-            hop(way, half - 1, s).wait_recv()
-            total = total + incoming[way, half - 1, s].astype(jnp.float32)
+            step = half - 1 - (early if way == 0 else 1 - early)
+            hop(way, step, s).wait_recv()
+            total = total + incoming[way, step, s].astype(jnp.float32)
         total_v[rows] = total
 
     for d in range(128):
         out_ref[0, :, d * 128 : (d + 1) * 128] = total_v[pl.ds(d, CSLOT, stride=128)]
 
-    for way in (0, 1):
-        @pl.loop(0, 8)
-        def _(s, way=way):
-            hop(way, half - 1, s).wait_send()
+    settle(1, True)
 
 
 def on_device(row_count, grp_count, a_blocks, prolong, a_cols, read_slots, agg, rap_slot):
@@ -218,16 +254,18 @@
     cap = read_slots.shape[1]
     half = grp_count // 2
     vmem = pl.BlockSpec(memory_space=pltpu.VMEM)
-    smem = pl.BlockSpec(memory_space=pltpu.SMEM)
-    hbm = pl.BlockSpec(memory_space=pl.ANY)
+    hbm = pl.BlockSpec(memory_space=pltpu.HBM)
     b16 = jnp.bfloat16
     dma = pltpu.SemaphoreType.DMA
     return pl.pallas_call(
         functools.partial(kernel, row_count, grp_count),
         out_shape=jax.ShapeDtypeStruct((1, CSLOT, coarse * coarse), jnp.float32),
-        in_specs=[vmem, smem, smem, smem, hbm, hbm],
+        in_specs=[hbm] * 6,
         out_specs=vmem,
         scratch_shapes=[
+            pltpu.SMEM(a_cols.shape[::-1], jnp.int32),
+            pltpu.SMEM(agg.shape, jnp.int32),
+            pltpu.SMEM(rap_slot.shape[::-1], jnp.int32),
             pltpu.VMEM((shard_rows, cells, width), b16),
             pltpu.VMEM((shard_rows, cells, coarse), b16),
             pltpu.VMEM((shard_rows + 2 * cap, cells, coarse), b16),
@@ -240,7 +278,7 @@
             pltpu.VMEM((2, cap, cells, coarse), b16),
             pltpu.VMEM((2, half, CSLOT, coarse, coarse), b16),
             pltpu.VMEM((2, half, CSLOT, coarse, coarse), b16),
-            dma((4,)),
+            dma((7,)),
             dma((2,)),
             dma((2,)),
             dma((2,)),

time: 56.5 us -> 56 us (level)
  no operation moved by 1% of the time
where the time goes in v3:
time: 56 us; the launch traced here: 55.8 us
  Pallas kernels  53.9 us (96%)
  local copies, waits for them, and re-layouts  1.87 us (3%)
    pallas_call x1, Pallas kernels, on_device(): pl.pallas_call(functools.partial(kernel, row_count, grp_count), out_shape...  53.9 us
    unnamed x1, local copies, waits for them, and re-layouts  1.87 us

profile of v3, /device:TPU:64, one launch (start us, length us, event | category | flops | bytes accessed | tf_op | source)
XLA Modules:
  0.0 55.8 jit_solution(4472496218111737152)
XLA Ops:
  0.0 53.9 %shard_map.64 = f32[1,8,16384]{2,1,0:T(8,128)} custom-call(s32[2,4]{1,0:T(2,128)} %reads_hbm.1, s32[8,48]{1,0:T(8,128)} %bitcast.2, s32[48]{0:T(128)} %agg_hbm.1, s32[8,48]{1,0:T(8,128)} %bitcast.3, bf16[48,64,512]{2,1,0:T(8,128)(2,1)} %a_hbm.1, bf16[48,64,128]{2,1,0:T(8,128)(2,1)} %p_hbm.1), custom_call_target="tpu_custom_call" | custom-call | tf_op jit(solution)/shard_map/pallas_call | solution.py:260
  53.9 1.9 %copy.8 = f32[1,8,16384]{2,1,0:T(8,128)} copy(f32[1,8,16384]{2,1,0:T(8,128)} %shard_map.64) | data formatting | bytes 1048576

commit v4 on v3

--- a/solution.py
+++ b/solution.py
@@ -25,7 +25,7 @@
     reads_hbm, cols_hbm, agg_hbm, rap_hbm, a_hbm, p_hbm,
     out_ref,
     cols_ref, agg_ref, rap_ref,
-    a_v, p_loc, p_all, p_turned, p_masked, near, total_v, req_v, req_s, stage, outgoing, incoming,
+    a_v, p_loc, p_all, p_turned, p_masked, near, terms_v, total_v, req_v, req_s, stage, outgoing, incoming,
     local_sem, req_send, req_recv, rep_send, rep_recv, ring_send, ring_recv,
 ):
     shard_rows, cells, _ = a_v.shape
@@ -146,106 +146,96 @@
     def _(i):
         slot_sums(i, first_half)
 
-    batch = shard_rows // 6
-
-    def later_sums(n):
-        @pl.loop(0, batch, unroll=min(4, batch))
-        def _(j):
-            slot_sums(n * batch + j, second_half)
-
-    def hop(way, step, s):
+    def hop(way, step, part):
         return pltpu.make_async_remote_copy(
-            src_ref=outgoing.at[way, step, s],
-            dst_ref=incoming.at[way, step, s],
-            send_sem=ring_send.at[way, step, s],
-            recv_sem=ring_recv.at[way, step, s],
+            src_ref=outgoing.at[way, step, part],
+            dst_ref=incoming.at[way, step, part],
+            send_sem=ring_send.at[way, step, part],
+            recv_sem=ring_recv.at[way, step, part],
             device_id={"grp": (ahead, behind)[way]},
             device_id_type=MESH,
         )
 
-    def own_terms(first, second, pair):
-        left = jnp.concatenate([p_masked[first], p_masked[second]], axis=0)
-        return jnp.dot(left, near[pair], preferred_element_type=jnp.float32)
-
-    def forward(way, step, pair, terms, receives):
-        for h in (0, 1):
-            s = pair * 2 + h
-            total = terms[:, h * 128 : (h + 1) * 128]
-            if receives:
-                hop(way, step - 1, s).wait_recv()
-                total = total + incoming[way, step - 1, s].astype(jnp.float32)
-            outgoing[way, step, s] = total.astype(jnp.bfloat16)
-            hop(way, step, s).start()
-
-    def advance(long_way, step, pair):
+    def advance(part, step, first=False, last=False):
         forth, back = half - step, grp_count - (half - 1 - step)
-        if long_way == 1:
+        if part == 1:
             forth, back = grp_count - forth, grp_count - back
-        last = isinstance(step, int) and step == half - 1
-        terms = own_terms(lax.rem(grp + forth, grp_count), lax.rem(grp + back, grp_count), pair)
-        receives = not (isinstance(step, int) and step == 0)
-        forward(long_way, step, pair, terms[:128], receives)
-        if last:
-            for h in (0, 1):
-                rows = pl.ds(pl.multiple_of((pair * 2 + h) * 128, 128), 128)
-                total_v[rows] = terms[128:, h * 128 : (h + 1) * 128]
-        else:
-            forward(1 - long_way, step, pair, terms[128:], receives)
-
-    @pl.loop(0, 2)
-    def _(n):
-        advance(0, 0, n)
-        later_sums(n)
-
-    @pl.loop(0, 2 * (half - 2))
-    def _(n):
-        advance(0, 1 + n // 2, n % 2)
-        if half > 2:
-            later_sums(2 + n)
-
-    for n in range(2 + 2 * (half - 2), 6):
-        later_sums(n)
-
-    @pl.loop(2, 4)
-    def _(pair):
-        advance(1, 0, pair)
-
-    @pl.loop(0, 2)
-    def _(pair):
-        advance(0, half - 1, pair)
-
-    @pl.loop(0, 2 * (half - 2))
-    def _(n):
-        advance(1, 1 + n // 2, 2 + n % 2)
-
-    @pl.loop(2, 4)
-    def _(pair):
-        advance(1, half - 1, pair)
-
-    def settle(way, long):
-        @pl.loop(0, 4 * (half if long else half - 1))
-        def _(n):
-            hop(way, n // 4, n % 4 + (4 if (way == 1) == long else 0)).wait_send()
-
-    settle(0, True)
-    settle(0, False)
-    settle(1, False)
-
-    @pl.loop(0, CSLOT)
-    def _(s):
-        rows = pl.ds(pl.multiple_of(s * 128, 128), 128)
-        total = total_v[rows]
-        early = s // 4
+        far, near_by = lax.rem(grp + forth, grp_count), lax.rem(grp + back, grp_count)
+
+        @pl.loop(0, 2)
+        def _(p):
+            left = jnp.concatenate([p_masked[far], p_masked[near_by]], axis=0)
+            terms_v[p] = jnp.dot(left, near[part * 2 + p], preferred_element_type=jnp.float32)
+
+        def term(side, slot):
+            lanes = slice(slot % 2 * 128, (slot % 2 + 1) * 128)
+            return terms_v[slot // 2, side * 128 : (side + 1) * 128, lanes]
+
+        for side, way in ((0, part), (1, 1 - part)):
+            if last and side == 1:
+                for slot in range(4):
+                    total_v[pl.ds((part * 4 + slot) * 128, 128)] = term(side, slot)
+                continue
+            if not first:
+                hop(way, step - 1, part).wait_recv()
+            for slot in range(4):
+                total = term(side, slot)
+                if not first:
+                    total = total + incoming[way, step - 1, part, slot].astype(jnp.float32)
+                outgoing[way, step, part, slot] = total.astype(jnp.bfloat16)
+            hop(way, step, part).start()
+
+    advance(0, 0, first=True)
+
+    @pl.loop(0, shard_rows, unroll=4)
+    def _(i):
+        slot_sums(i, second_half)
+
+    advance(1, 0, first=True)
+
+    @pl.loop(1, half - 1)
+    def _(step):
+        advance(0, step)
+        advance(1, step)
+
+    advance(0, half - 1, last=True)
+    advance(1, half - 1, last=True)
+
+    for step in range(half - 1):
         for way in (0, 1):
-            step = half - 1 - (early if way == 0 else 1 - early)
-            hop(way, step, s).wait_recv()
-            total = total + incoming[way, step, s].astype(jnp.float32)
-        total_v[rows] = total
+            for part in (0, 1):
+                hop(way, step, part).wait_send()
+
+    for part in (0, 1):
+        hop(part, half - 1, part).wait_recv()
+        hop(1 - part, half - 2, part).wait_recv()
+        for slot in range(4):
+            rows = pl.ds((part * 4 + slot) * 128, 128)
+            total_v[rows] = (
+                total_v[rows]
+                + incoming[part, half - 1, part, slot].astype(jnp.float32)
+                + incoming[1 - part, half - 2, part, slot].astype(jnp.float32)
+            )
 
     for d in range(128):
         out_ref[0, :, d * 128 : (d + 1) * 128] = total_v[pl.ds(d, CSLOT, stride=128)]
 
-    settle(1, True)
+    for part in (0, 1):
+        hop(part, half - 1, part).wait_send()
+
+
+def move(source, target, sems):
+    width = source.shape[2] // 4
+    copies = [
+        pltpu.make_async_copy(
+            source.at[:, :, pl.ds(n * width, width)], target.at[:, :, pl.ds(n * width, width)], sems.at[n]
+        )
+        for n in range(4)
+    ]
+    for copy in copies:
+        copy.start()
+    for copy in copies:
+        copy.wait()
 
 
 def on_device(row_count, grp_count, a_blocks, prolong, a_cols, read_slots, agg, rap_slot):
@@ -257,7 +247,7 @@
     hbm = pl.BlockSpec(memory_space=pltpu.HBM)
     b16 = jnp.bfloat16
     dma = pltpu.SemaphoreType.DMA
-    return pl.pallas_call(
+    out = pl.pallas_call(
         functools.partial(kernel, row_count, grp_count),
         out_shape=jax.ShapeDtypeStruct((1, CSLOT, coarse * coarse), jnp.float32),
         in_specs=[hbm] * 6,
@@ -272,24 +262,33 @@
             pltpu.VMEM((coarse, shard_rows * cells), b16),
             pltpu.VMEM((grp_count, coarse, shard_rows * cells), b16),
             pltpu.VMEM((CSLOT // 2, shard_rows * cells, 2 * coarse), b16),
+            pltpu.VMEM((2, 2 * coarse, 2 * coarse), jnp.float32),
             pltpu.VMEM((CSLOT * coarse, coarse), jnp.float32),
             pltpu.VMEM((2, 2, cap), jnp.int32),
             pltpu.SMEM((2, 2, cap), jnp.int32),
             pltpu.VMEM((2, cap, cells, coarse), b16),
-            pltpu.VMEM((2, half, CSLOT, coarse, coarse), b16),
-            pltpu.VMEM((2, half, CSLOT, coarse, coarse), b16),
+            pltpu.VMEM((2, half, 2, CSLOT // 2, coarse, coarse), b16),
+            pltpu.VMEM((2, half, 2, CSLOT // 2, coarse, coarse), b16),
             dma((7,)),
             dma((2,)),
             dma((2,)),
             dma((2,)),
             dma((2,)),
-            dma((2, half, CSLOT)),
-            dma((2, half, CSLOT)),
+            dma((2, half, 2)),
+            dma((2, half, 2)),
         ],
         compiler_params=pltpu.CompilerParams(
             collective_id=0, has_side_effects=True, vmem_limit_bytes=56 * 1024 * 1024
         ),
     )(read_slots, a_cols.T, agg, rap_slot.T, a_blocks, prolong)
+    return pl.pallas_call(
+        move,
+        out_shape=jax.ShapeDtypeStruct(out.shape, out.dtype),
+        in_specs=[hbm],
+        out_specs=hbm,
+        scratch_shapes=[dma((4,))],
+        compiler_params=pltpu.CompilerParams(vmem_limit_bytes=56 * 1024 * 1024),
+    )(out)
 
 
 def solution(mesh):

time: 56 us -> 70 us (1.25)
  Pallas kernels: 53.9 us -> 69.9 us
  local copies, waits for them, and re-layouts: 1.87 us -> 0 us
    pallas_call x0 -> x1, Pallas kernels: none -> 17 us  [on_device(): pl.pallas_call(move, out_shape=jax.ShapeDtypeStruct(out.shape, out.dtype)...]
    unnamed x1 -> x0, local copies, waits for them, and re-layouts: 1.87 us -> none
    pallas_call x1, Pallas kernels: 53.9 us -> 52.8 us  [on_device(): pl.pallas_call(functools.partial(kernel, row_count, grp_count), out_shape...]
where the time goes in v4:
time: 70 us; the launch traced here: 69.9 us
  Pallas kernels  69.9 us (100%)
    pallas_call x1, Pallas kernels, on_device(): pl.pallas_call(functools.partial(kernel, row_count, grp_count), out_shape...  52.8 us
    pallas_call x1, Pallas kernels, on_device(): pl.pallas_call(move, out_shape=jax.ShapeDtypeStruct(out.shape, out.dtype)...  17 us

profile of v4, /device:TPU:64, one launch (start us, length us, event | category | flops | bytes accessed | tf_op | source)
XLA Modules:
  0.0 69.9 jit_solution(9443081001728600224)
XLA Ops:
  0.0 52.8 %shard_map.64.source = f32[1,8,16384]{2,1,0:T(8,128)} custom-call(s32[2,4]{1,0:T(2,128)} %reads_hbm.1, s32[8,48]{1,0:T(8,128)} %bitcast.2, s32[48]{0:T(128)} %agg_hbm.1, s32[8,48]{1,0:T(8,128)} %bitcast.3, bf16[48,64,512]{2,1,0:T(8,128)(2,1)} %a_hbm.1, bf16[48,64,128]{2,1,0:T(8,128)(2,1)} %p_hbm.1), custom_call_target="tpu_custom_call" | custom-call | tf_op jit(solution)/shard_map/pallas_call | solution.py:250
  52.8 17.0 %shard_map.65 = f32[1,8,16384]{2,1,0:T(8,128)} custom-call(f32[1,8,16384]{2,1,0:T(8,128)} %shard_map.64.source), custom_call_target="tpu_custom_call" | custom-call | tf_op jit(solution)/shard_map/pallas_call | solution.py:284

commit v5 on v4

v5 whole, which is shorter than its diff:
```python
import functools

import jax
import jax.numpy as jnp
from jax import lax
from jax.experimental import pallas as pl
from jax.experimental.pallas import tpu as pltpu
from jax.sharding import PartitionSpec as P

CSLOT = 8
MESH = pl.DeviceIdType.MESH


def lane_pair(left, right, rows):
    lanes = lax.broadcasted_iota(jnp.int32, (rows, 128), 1)
    return jnp.where(lanes < 64, left, right)


def indicator(value, wanted):
    return jnp.where(value == wanted, 1.0, 0.0).astype(jnp.bfloat16)


def kernel(
    row_count, grp_count,
    reads_hbm, cols_hbm, agg_hbm, rap_hbm, a_hbm, p_hbm,
    out_ref,
    cols_ref, agg_ref, rap_ref,
    a_v, p_loc, p_all, left, near, sums, order_v, order_s, keep_s, last_s, total_v, req_v, req_s, stage, outgoing, incoming,
    local_sem, req_send, req_recv, rep_send, rep_recv, ring_send, ring_recv,
):
    shard_rows, cells, _ = a_v.shape
    slot_count = cols_ref.shape[0]
    cap = stage.shape[1]
    half = grp_count // 2
    chunk_count = left.shape[0]
    row, grp = lax.axis_index("rows"), lax.axis_index("grp")
    above, below = lax.rem(row + 1, row_count), lax.rem(row + row_count - 1, row_count)
    ahead, behind = lax.rem(grp + 1, grp_count), lax.rem(grp + grp_count - 1, grp_count)

    a_copy = pltpu.make_async_copy(a_hbm, a_v, local_sem.at[0])
    p_copy = pltpu.make_async_copy(p_hbm, p_loc.at[pl.ds(0, shard_rows)], local_sem.at[1])
    all_copy = pltpu.make_async_copy(p_hbm, p_all.at[pl.ds(0, shard_rows)], local_sem.at[2])
    p_copy.start()
    a_copy.start()
    all_copy.start()
    index_copies = [
        pltpu.make_async_copy(source, target, local_sem.at[4 + n])
        for n, (source, target) in enumerate(
            ((agg_hbm, agg_ref), (cols_hbm, cols_ref), (rap_hbm, rap_ref))
        )
    ]
    for copy in index_copies:
        copy.start()

    barrier = pltpu.get_barrier_semaphore()
    for device in ({"rows": above}, {"rows": below}, {"grp": ahead}, {"grp": behind}):
        pl.semaphore_signal(barrier, inc=1, device_id=device, device_id_type=MESH)
    pl.semaphore_wait(barrier, 4)

    def request(side):
        return pltpu.make_async_remote_copy(
            src_ref=reads_hbm,
            dst_ref=req_v.at[1 - side],
            send_sem=req_send.at[side],
            recv_sem=req_recv.at[1 - side],
            device_id={"rows": (below, above)[side]},
            device_id_type=MESH,
        )

    def reply(side):
        return pltpu.make_async_remote_copy(
            src_ref=stage.at[side],
            dst_ref=p_all.at[pl.ds(shard_rows + (1 - side) * cap, cap)],
            send_sem=rep_send.at[side],
            recv_sem=rep_recv.at[1 - side],
            device_id={"rows": (below, above)[side]},
            device_id_type=MESH,
        )

    for side in (0, 1):
        request(side).start()

    p_copy.wait()
    p_loc[shard_rows] = jnp.zeros(p_loc.shape[1:], p_loc.dtype)
    for side in (0, 1):
        request(side).wait()
    req_copy = pltpu.make_async_copy(req_v, req_s, local_sem.at[3])
    req_copy.start()
    req_copy.wait()
    for side in (0, 1):
        for c in range(cap):
            stage[side, c] = p_loc[jnp.maximum(req_s[side, 1 - side, c], 0)]
        reply(side).start()

    index_copies[0].wait()

    def count(i, counts):
        return tuple(n + (agg_ref[i] == q).astype(jnp.int32) for q, n in enumerate(counts))

    counts = lax.fori_loop(0, shard_rows, count, (jnp.int32(0),) * grp_count)
    starts = [jnp.int32(0)]
    for n in counts:
        starts.append(starts[-1] + (n + 3) // 4)
    for q in range(grp_count):
        last_s[q] = jnp.where(counts[q] > 0, starts[q + 1], 0)
    for j in range(chunk_count):
        begins = jnp.int32(0)
        for q in range(grp_count):
            begins = jnp.where((starts[q] == j) & (counts[q] > 0), 1, begins)
        keep_s[j] = 1 - begins
    lanes = lax.broadcasted_iota(jnp.int32, order_v.shape, 1)

    def place(i, carry):
        heads, order = carry
        spot = jnp.int32(0)
        for q, head in enumerate(heads):
            spot = jnp.where(agg_ref[i] == q, head, spot)
        heads = tuple(head + (agg_ref[i] == q).astype(jnp.int32) for q, head in enumerate(heads))
        return heads, jnp.where(lanes == spot, i, order)

    heads = tuple(start * 4 for start in starts[:-1])
    _, order = lax.fori_loop(
        0, shard_rows, place, (heads, jnp.full(order_v.shape, shard_rows, jnp.int32))
    )
    order_v[...] = order
    order_copy = pltpu.make_async_copy(order_v, order_s, local_sem.at[7])
    order_copy.start()
    for copy in index_copies[1:]:
        copy.wait()
    order_copy.wait()

    @pl.loop(0, chunk_count, unroll=2)
    def _(j):
        blocks = [p_loc[order_s[0, 4 * j + n]] for n in range(4)]
        left[j] = jnp.concatenate(blocks, axis=0).T

    for part in (0, 1):
        sums[part, 0] = jnp.zeros(sums.shape[2:], jnp.float32)

    a_copy.wait()
    all_copy.wait()
    for side in (0, 1):
        reply(side).wait()

    def slot_sums(i, slots):
        columns = jnp.concatenate(
            [p_all[jnp.maximum(cols_ref[k, i], 0)] for k in range(slot_count)], axis=0
        )
        places = [
            jnp.where(cols_ref[k, i] >= 0, rap_ref[k, i], -1) for k in range(slot_count)
        ]
        spread = []
        for k in range(0, slot_count, 2):
            block = a_v[i, :, k * cells : (k + 2) * cells]
            place = lane_pair(places[k], places[k + 1], 16)
            keeps = [indicator(place, s) for s in slots]
            spread.append(
                jnp.concatenate(
                    [block * jnp.concatenate([keep] * (cells // 16), axis=0) for keep in keeps],
                    axis=0,
                )
            )
        product = jnp.dot(
            jnp.concatenate(spread, axis=1), columns, preferred_element_type=jnp.float32
        ).astype(jnp.bfloat16)
        for n, s in enumerate(slots):
            near[s // 4, i, :, s % 4 * 128 : (s % 4 + 1) * 128] = product[
                n * cells : (n + 1) * cells
            ]

    def chunk_sums(part):
        @pl.loop(0, chunk_count, unroll=2)
        def _(j):
            rows = [jnp.minimum(order_s[0, 4 * j + n], shard_rows - 1) for n in range(4)]
            right = jnp.concatenate([near[part, row] for row in rows], axis=0)
            keep = keep_s[j].astype(jnp.float32)
            sums[part, j + 1] = sums[part, j] * keep + jnp.dot(
                left[j], right, preferred_element_type=jnp.float32
            )

    first_half, second_half = range(CSLOT // 2), range(CSLOT // 2, CSLOT)

    @pl.loop(0, shard_rows, unroll=4)
    def _(i):
        slot_sums(i, first_half)

    chunk_sums(0)

    def hop(way, step, part, pair):
        return pltpu.make_async_remote_copy(
            src_ref=outgoing.at[way, step, part, pair],
            dst_ref=incoming.at[way, step, part, pair],
            send_sem=ring_send.at[way, step, part, pair],
            recv_sem=ring_recv.at[way, step, part, pair],
            device_id={"grp": (ahead, behind)[way]},
            device_id_type=MESH,
        )

    def term(part, q, slot):
        return sums[part, last_s[q], :, slot * 128 : (slot + 1) * 128]

    def advance(part, step):
        forth, back = half - step, grp_count - (half - 1 - step)
        if part == 1:
            forth, back = grp_count - forth, grp_count - back
        for pair in (0, 1):
            for away, way in ((forth, part), (back, 1 - part)):
                if way != part and step == half - 1:
                    continue
                q = lax.rem(grp + away, grp_count)
                if step > 0:
                    hop(way, step - 1, part, pair).wait_recv()
                for h in (0, 1):
                    total = term(part, q, pair * 2 + h)
                    if step > 0:
                        total = total + incoming[way, step - 1, part, pair, h].astype(jnp.float32)
                    outgoing[way, step, part, pair, h] = total.astype(jnp.bfloat16)
                hop(way, step, part, pair).start()

    def later_sums(first, end):
        @pl.loop(first, end, unroll=4)
        def _(i):
            slot_sums(i, second_half)

    advance(0, 0)
    later_sums(0, shard_rows // 2)
    if half > 2:
        advance(0, 1)
    later_sums(shard_rows // 2, shard_rows)
    chunk_sums(1)
    advance(1, 0)
    for step in range(2 if half > 2 else 1, half):
        advance(0, step)
        advance(1, step - 1)
    advance(1, half - 1)

    for way in (0, 1):
        for step in range(half - 1):
            for part in (0, 1):
                for pair in (0, 1):
                    hop(way, step, part, pair).wait_send()

    for part in (0, 1):
        for pair in (0, 1):
            hop(part, half - 1, part, pair).wait_recv()
            hop(1 - part, half - 2, part, pair).wait_recv()
            for h in (0, 1):
                slot = pair * 2 + h
                total_v[pl.ds((part * 4 + slot) * 128, 128)] = (
                    term(part, grp, slot)
                    + incoming[part, half - 1, part, pair, h].astype(jnp.float32)
                    + incoming[1 - part, half - 2, part, pair, h].astype(jnp.float32)
                )

    for d in range(128):
        out_ref[0, :, d * 128 : (d + 1) * 128] = total_v[pl.ds(d, CSLOT, stride=128)]

    for part in (0, 1):
        for pair in (0, 1):
            hop(part, half - 1, part, pair).wait_send()


def on_device(row_count, grp_count, a_blocks, prolong, a_cols, read_slots, agg, rap_slot):
    shard_rows, cells, width = a_blocks.shape
    coarse = prolong.shape[2]
    cap = read_slots.shape[1]
    half = grp_count // 2
    chunk_count = (shard_rows + 3 * grp_count) // 4
    vmem = pl.BlockSpec(memory_space=pltpu.VMEM)
    hbm = pl.BlockSpec(memory_space=pltpu.HBM)
    b16 = jnp.bfloat16
    dma = pltpu.SemaphoreType.DMA
    return pl.pallas_call(
        functools.partial(kernel, row_count, grp_count),
        out_shape=jax.ShapeDtypeStruct((1, CSLOT, coarse * coarse), jnp.float32),
        in_specs=[hbm] * 6,
        out_specs=vmem,
        scratch_shapes=[
            pltpu.SMEM(a_cols.shape[::-1], jnp.int32),
            pltpu.SMEM(agg.shape, jnp.int32),
            pltpu.SMEM(rap_slot.shape[::-1], jnp.int32),
            pltpu.VMEM((shard_rows, cells, width), b16),
            pltpu.VMEM((shard_rows + 1, cells, coarse), b16),
            pltpu.VMEM((shard_rows + 2 * cap, cells, coarse), b16),
            pltpu.VMEM((chunk_count, coarse, 4 * cells), b16),
            pltpu.VMEM((2, shard_rows, cells, CSLOT // 2 * coarse), b16),
            pltpu.VMEM((2, chunk_count + 1, coarse, CSLOT // 2 * coarse), jnp.float32),
            pltpu.VMEM((8, 128), jnp.int32),
            pltpu.SMEM((8, 128), jnp.int32),
            pltpu.SMEM((chunk_count,), jnp.int32),
            pltpu.SMEM((grp_count,), jnp.int32),
            pltpu.VMEM((CSLOT * coarse, coarse), jnp.float32),
            pltpu.VMEM((2, 2, cap), jnp.int32),
            pltpu.SMEM((2, 2, cap), jnp.int32),
            pltpu.VMEM((2, cap, cells, coarse), b16),
            pltpu.VMEM((2, half, 2, 2, 2, coarse, coarse), b16),
            pltpu.VMEM((2, half, 2, 2, 2, coarse, coarse), b16),
            dma((8,)),
            dma((2,)),
            dma((2,)),
            dma((2,)),
            dma((2,)),
            dma((2, half, 2, 2)),
            dma((2, half, 2, 2)),
        ],
        compiler_params=pltpu.CompilerParams(
            collective_id=0, has_side_effects=True, vmem_limit_bytes=56 * 1024 * 1024
        ),
    )(read_slots, a_cols.T, agg, rap_slot.T, a_blocks, prolong)

def solution(mesh):
    return jax.shard_map(
        functools.partial(on_device, mesh.shape["rows"], mesh.shape["grp"]),
        mesh=mesh,
        in_specs=(
            P(("rows", "grp"), None, None),
            P(("rows", "grp"), None, None),
            P(("rows", "grp"), None),
            P(("rows", "grp"), None),
            P(("rows", "grp")),
            P(("rows", "grp"), None),
        ),
        out_specs=P(("rows", "grp"), None, None),
        check_vma=False,
    )
```

time: 70 us -> 55.7 us (0.80)
  Pallas kernels: 69.9 us -> 53.6 us
  local copies, waits for them, and re-layouts: 0 us -> 1.87 us
    pallas_call x1 -> x0, Pallas kernels: 17 us -> none  [on_device(): pl.pallas_call(move, out_shape=jax.ShapeDtypeStruct(out.shape, out.dtype)...]
    unnamed x0 -> x1, local copies, waits for them, and re-layouts: none -> 1.87 us
    pallas_call x1, Pallas kernels: 52.8 us -> 53.6 us  [on_device(): pl.pallas_call(functools.partial(kernel, row_count, grp_count), out_shape...]
where the time goes in v5:
time: 55.7 us; the launch traced here: 55.5 us
  Pallas kernels  53.6 us (96%)
  local copies, waits for them, and re-layouts  1.87 us (3%)
    pallas_call x1, Pallas kernels, on_device(): pl.pallas_call(functools.partial(kernel, row_count, grp_count), out_shape...  53.6 us
    unnamed x1, local copies, waits for them, and re-layouts  1.87 us

profile of v5, /device:TPU:64, one launch (start us, length us, event | category | flops | bytes accessed | tf_op | source)
XLA Modules:
  0.0 55.5 jit_solution(9980564043191581413)
XLA Ops:
  0.0 53.6 %shard_map.64 = f32[1,8,16384]{2,1,0:T(8,128)} custom-call(s32[2,4]{1,0:T(2,128)} %reads_hbm.1, s32[8,48]{1,0:T(8,128)} %bitcast.2, s32[48]{0:T(128)} %agg_hbm.1, s32[8,48]{1,0:T(8,128)} %bitcast.3, bf16[48,64,512]{2,1,0:T(8,128)(2,1)} %a_hbm.1, bf16[48,64,128]{2,1,0:T(8,128)(2,1)} %p_hbm.1), custom_call_target="tpu_custom_call" | custom-call | tf_op jit(solution)/shard_map/pallas_call | solution.py:273
  53.6 1.9 %copy.8 = f32[1,8,16384]{2,1,0:T(8,128)} copy(f32[1,8,16384]{2,1,0:T(8,128)} %shard_map.64) | data formatting | bytes 1048576

commit v6 on v5

--- a/solution.py
+++ b/solution.py
@@ -35,7 +35,8 @@
     chunk_count = left.shape[0]
     row, grp = lax.axis_index("rows"), lax.axis_index("grp")
     above, below = lax.rem(row + 1, row_count), lax.rem(row + row_count - 1, row_count)
-    ahead, behind = lax.rem(grp + 1, grp_count), lax.rem(grp + grp_count - 1, grp_count)
+    turn = 1 - 2 * lax.rem(row, 2)
+    ahead, behind = (lax.rem(grp + sign * turn + grp_count, grp_count) for sign in (1, -1))
 
     a_copy = pltpu.make_async_copy(a_hbm, a_v, local_sem.at[0])
     p_copy = pltpu.make_async_copy(p_hbm, p_loc.at[pl.ds(0, shard_rows)], local_sem.at[1])
@@ -200,14 +201,13 @@
         return sums[part, last_s[q], :, slot * 128 : (slot + 1) * 128]
 
     def advance(part, step):
-        forth, back = half - step, grp_count - (half - 1 - step)
-        if part == 1:
-            forth, back = grp_count - forth, grp_count - back
+        sign = 1 - 2 * part
+        forth, back = sign * (half - step), -sign * (half - 1 - step)
         for pair in (0, 1):
             for away, way in ((forth, part), (back, 1 - part)):
                 if way != part and step == half - 1:
                     continue
-                q = lax.rem(grp + away, grp_count)
+                q = lax.rem(grp + turn * away + grp_count, grp_count)
                 if step > 0:
                     hop(way, step - 1, part, pair).wait_recv()
                 for h in (0, 1):

time: 55.7 us -> 57 us (1.023)
  Pallas kernels: 53.6 us -> 55 us
    pallas_call x1, Pallas kernels: 53.6 us -> 55 us  [on_device(): pl.pallas_call(functools.partial(kernel, row_count, grp_count), out_shape...]
where the time goes in v6:
time: 57 us; the launch traced here: 56.9 us
  Pallas kernels  55 us (96%)
  local copies, waits for them, and re-layouts  1.87 us (3%)
    pallas_call x1, Pallas kernels, on_device(): pl.pallas_call(functools.partial(kernel, row_count, grp_count), out_shape...  55 us
    unnamed x1, local copies, waits for them, and re-layouts  1.87 us

profile of v6, /device:TPU:64, one launch (start us, length us, event | category | flops | bytes accessed | tf_op | source)
XLA Modules:
  0.0 56.9 jit_solution(14791331512814192154)
XLA Ops:
  0.0 55.0 %shard_map.64 = f32[1,8,16384]{2,1,0:T(8,128)} custom-call(s32[2,4]{1,0:T(2,128)} %reads_hbm.1, s32[8,48]{1,0:T(8,128)} %bitcast.2, s32[48]{0:T(128)} %agg_hbm.1, s32[8,48]{1,0:T(8,128)} %bitcast.3, bf16[48,64,512]{2,1,0:T(8,128)(2,1)} %a_hbm.1, bf16[48,64,128]{2,1,0:T(8,128)(2,1)} %p_hbm.1), custom_call_target="tpu_custom_call" | custom-call | tf_op jit(solution)/shard_map/pallas_call | solution.py:273
  55.0 1.9 %copy.8 = f32[1,8,16384]{2,1,0:T(8,128)} copy(f32[1,8,16384]{2,1,0:T(8,128)} %shard_map.64) | data formatting | bytes 1048576

commit v7 on v4

--- a/solution.py
+++ b/solution.py
@@ -25,7 +25,7 @@
     reads_hbm, cols_hbm, agg_hbm, rap_hbm, a_hbm, p_hbm,
     out_ref,
     cols_ref, agg_ref, rap_ref,
-    a_v, p_loc, p_all, p_turned, p_masked, near, terms_v, total_v, req_v, req_s, stage, outgoing, incoming,
+    a_v, p_loc, p_all, p_turned, p_masked, near, total_v, req_v, req_s, stage, outgoing, incoming,
     local_sem, req_send, req_recv, rep_send, rep_recv, ring_send, ring_recv,
 ):
     shard_rows, cells, _ = a_v.shape
@@ -140,102 +140,87 @@
                 n * cells : (n + 1) * cells
             ]
 
-    first_half, second_half = range(CSLOT // 2), range(CSLOT // 2, CSLOT)
-
-    @pl.loop(0, shard_rows, unroll=4)
-    def _(i):
-        slot_sums(i, first_half)
-
-    def hop(way, step, part):
+    def quarter(pair):
+        @pl.loop(0, shard_rows, unroll=min(8, shard_rows))
+        def _(i):
+            slot_sums(i, (2 * pair, 2 * pair + 1))
+
+    def hop(way, step, part, pair):
         return pltpu.make_async_remote_copy(
-            src_ref=outgoing.at[way, step, part],
-            dst_ref=incoming.at[way, step, part],
-            send_sem=ring_send.at[way, step, part],
-            recv_sem=ring_recv.at[way, step, part],
+            src_ref=outgoing.at[way, step, part, pair],
+            dst_ref=incoming.at[way, step, part, pair],
+            send_sem=ring_send.at[way, step, part, pair],
+            recv_sem=ring_recv.at[way, step, part, pair],
             device_id={"grp": (ahead, behind)[way]},
             device_id_type=MESH,
         )
 
-    def advance(part, step, first=False, last=False):
+    def advance(part, step, pair):
         forth, back = half - step, grp_count - (half - 1 - step)
         if part == 1:
             forth, back = grp_count - forth, grp_count - back
         far, near_by = lax.rem(grp + forth, grp_count), lax.rem(grp + back, grp_count)
-
+        left = jnp.concatenate([p_masked[far], p_masked[near_by]], axis=0)
+        terms = jnp.dot(left, near[part * 2 + pair], preferred_element_type=jnp.float32)
+        for side, way in ((0, part), (1, 1 - part)):
+            last = side == 1 and step == half - 1
+            if step > 0 and not last:
+                hop(way, step - 1, part, pair).wait_recv()
+            for h in (0, 1):
+                total = terms[side * 128 : (side + 1) * 128, h * 128 : (h + 1) * 128]
+                if last:
+                    slot = part * 4 + pair * 2 + h
+                    total_v[pl.ds(pl.multiple_of(slot * 128, 128), 128)] = total
+                    continue
+                if step > 0:
+                    total = total + incoming[way, step - 1, part, pair, h].astype(jnp.float32)
+                outgoing[way, step, part, pair, h] = total.astype(jnp.bfloat16)
+            if not last:
+                hop(way, step, part, pair).start()
+
+    def advance_both(part, step):
         @pl.loop(0, 2)
-        def _(p):
-            left = jnp.concatenate([p_masked[far], p_masked[near_by]], axis=0)
-            terms_v[p] = jnp.dot(left, near[part * 2 + p], preferred_element_type=jnp.float32)
-
-        def term(side, slot):
-            lanes = slice(slot % 2 * 128, (slot % 2 + 1) * 128)
-            return terms_v[slot // 2, side * 128 : (side + 1) * 128, lanes]
-
-        for side, way in ((0, part), (1, 1 - part)):
-            if last and side == 1:
-                for slot in range(4):
-                    total_v[pl.ds((part * 4 + slot) * 128, 128)] = term(side, slot)
-                continue
-            if not first:
-                hop(way, step - 1, part).wait_recv()
-            for slot in range(4):
-                total = term(side, slot)
-                if not first:
-                    total = total + incoming[way, step - 1, part, slot].astype(jnp.float32)
-                outgoing[way, step, part, slot] = total.astype(jnp.bfloat16)
-            hop(way, step, part).start()
-
-    advance(0, 0, first=True)
-
-    @pl.loop(0, shard_rows, unroll=4)
-    def _(i):
-        slot_sums(i, second_half)
-
-    advance(1, 0, first=True)
-
-    @pl.loop(1, half - 1)
-    def _(step):
-        advance(0, step)
-        advance(1, step)
-
-    advance(0, half - 1, last=True)
-    advance(1, half - 1, last=True)
-
-    for step in range(half - 1):
-        for way in (0, 1):
+        def _(pair):
+            advance(part, step, pair)
+
+    quarter(0)
+    advance(0, 0, 0)
+    quarter(1)
+    advance(0, 0, 1)
+    advance(0, 1, 0)
+    quarter(2)
+    advance(0, 1, 1)
+    quarter(3)
+    advance_both(1, 0)
+    for step in range(2, half):
+        advance_both(0, step)
+        advance_both(1, step - 1)
+    advance_both(1, half - 1)
+
+    for way in (0, 1):
+        for step in range(half - 1):
             for part in (0, 1):
-                hop(way, step, part).wait_send()
+                for pair in (0, 1):
+                    hop(way, step, part, pair).wait_send()
 
     for part in (0, 1):
-        hop(part, half - 1, part).wait_recv()
-        hop(1 - part, half - 2, part).wait_recv()
-        for slot in range(4):
-            rows = pl.ds((part * 4 + slot) * 128, 128)
-            total_v[rows] = (
-                total_v[rows]
-                + incoming[part, half - 1, part, slot].astype(jnp.float32)
-                + incoming[1 - part, half - 2, part, slot].astype(jnp.float32)
-            )
+        for pair in (0, 1):
+            hop(part, half - 1, part, pair).wait_recv()
+            hop(1 - part, half - 2, part, pair).wait_recv()
+            for h in (0, 1):
+                rows = pl.ds((part * 4 + pair * 2 + h) * 128, 128)
+                total_v[rows] = (
+                    total_v[rows]
+                    + incoming[part, half - 1, part, pair, h].astype(jnp.float32)
+                    + incoming[1 - part, half - 2, part, pair, h].astype(jnp.float32)
+                )
 
     for d in range(128):
         out_ref[0, :, d * 128 : (d + 1) * 128] = total_v[pl.ds(d, CSLOT, stride=128)]
 
     for part in (0, 1):
-        hop(part, half - 1, part).wait_send()
-
-
-def move(source, target, sems):
-    width = source.shape[2] // 4
-    copies = [
-        pltpu.make_async_copy(
-            source.at[:, :, pl.ds(n * width, width)], target.at[:, :, pl.ds(n * width, width)], sems.at[n]
-        )
-        for n in range(4)
-    ]
-    for copy in copies:
-        copy.start()
-    for copy in copies:
-        copy.wait()
+        for pair in (0, 1):
+            hop(part, half - 1, part, pair).wait_send()
 
 
 def on_device(row_count, grp_count, a_blocks, prolong, a_cols, read_slots, agg, rap_slot):
@@ -247,7 +232,7 @@
     hbm = pl.BlockSpec(memory_space=pltpu.HBM)
     b16 = jnp.bfloat16
     dma = pltpu.SemaphoreType.DMA
-    out = pl.pallas_call(
+    return pl.pallas_call(
         functools.partial(kernel, row_count, grp_count),
         out_shape=jax.ShapeDtypeStruct((1, CSLOT, coarse * coarse), jnp.float32),
         in_specs=[hbm] * 6,
@@ -262,34 +247,24 @@
             pltpu.VMEM((coarse, shard_rows * cells), b16),
             pltpu.VMEM((grp_count, coarse, shard_rows * cells), b16),
             pltpu.VMEM((CSLOT // 2, shard_rows * cells, 2 * coarse), b16),
-            pltpu.VMEM((2, 2 * coarse, 2 * coarse), jnp.float32),
             pltpu.VMEM((CSLOT * coarse, coarse), jnp.float32),
             pltpu.VMEM((2, 2, cap), jnp.int32),
             pltpu.SMEM((2, 2, cap), jnp.int32),
             pltpu.VMEM((2, cap, cells, coarse), b16),
-            pltpu.VMEM((2, half, 2, CSLOT // 2, coarse, coarse), b16),
-            pltpu.VMEM((2, half, 2, CSLOT // 2, coarse, coarse), b16),
+            pltpu.VMEM((2, half, 2, 2, 2, coarse, coarse), b16),
+            pltpu.VMEM((2, half, 2, 2, 2, coarse, coarse), b16),
             dma((7,)),
             dma((2,)),
             dma((2,)),
             dma((2,)),
             dma((2,)),
-            dma((2, half, 2)),
-            dma((2, half, 2)),
+            dma((2, half, 2, 2)),
+            dma((2, half, 2, 2)),
         ],
         compiler_params=pltpu.CompilerParams(
             collective_id=0, has_side_effects=True, vmem_limit_bytes=56 * 1024 * 1024
         ),
     )(read_slots, a_cols.T, agg, rap_slot.T, a_blocks, prolong)
-    return pl.pallas_call(
-        move,
-        out_shape=jax.ShapeDtypeStruct(out.shape, out.dtype),
-        in_specs=[hbm],
-        out_specs=hbm,
-        scratch_shapes=[dma((4,))],
-        compiler_params=pltpu.CompilerParams(vmem_limit_bytes=56 * 1024 * 1024),
-    )(out)
-
 
 def solution(mesh):
     return jax.shard_map(

time: 70 us -> 53.5 us (0.76)
  Pallas kernels: 69.9 us -> 51.5 us
  local copies, waits for them, and re-layouts: 0 us -> 1.87 us
    pallas_call x1 -> x0, Pallas kernels: 17 us -> none  [on_device(): pl.pallas_call(move, out_shape=jax.ShapeDtypeStruct(out.shape, out.dtype)...]
    unnamed x0 -> x1, local copies, waits for them, and re-layouts: none -> 1.87 us
    pallas_call x1, Pallas kernels: 52.8 us -> 51.5 us  [on_device(): pl.pallas_call(functools.partial(kernel, row_count, grp_count), out_shape...]
where the time goes in v7:
time: 53.5 us; the launch traced here: 53.4 us
  Pallas kernels  51.5 us (96%)
  local copies, waits for them, and re-layouts  1.87 us (3%)
    pallas_call x1, Pallas kernels, on_device(): pl.pallas_call(functools.partial(kernel, row_count, grp_count), out_shape...  51.5 us
    unnamed x1, local copies, waits for them, and re-layouts  1.87 us

profile of v7, /device:TPU:64, one launch (start us, length us, event | category | flops | bytes accessed | tf_op | source)
XLA Modules:
  0.0 53.4 jit_solution(3665529505361191115)
XLA Ops:
  0.0 51.5 %shard_map.64 = f32[1,8,16384]{2,1,0:T(8,128)} custom-call(s32[2,4]{1,0:T(2,128)} %reads_hbm.1, s32[8,48]{1,0:T(8,128)} %bitcast.2, s32[48]{0:T(128)} %agg_hbm.1, s32[8,48]{1,0:T(8,128)} %bitcast.3, bf16[48,64,512]{2,1,0:T(8,128)(2,1)} %a_hbm.1, bf16[48,64,128]{2,1,0:T(8,128)(2,1)} %p_hbm.1), custom_call_target="tpu_custom_call" | custom-call | tf_op jit(solution)/shard_map/pallas_call | solution.py:235
  51.5 1.9 %copy.8 = f32[1,8,16384]{2,1,0:T(8,128)} copy(f32[1,8,16384]{2,1,0:T(8,128)} %shard_map.64) | data formatting | bytes 1048576

commit v8 on v7

--- a/solution.py
+++ b/solution.py
@@ -81,32 +81,38 @@
 
     p_copy.wait()
 
+    for side in (0, 1):
+        request(side).wait()
+    req_copy = pltpu.make_async_copy(req_v, req_s, local_sem.at[3])
+    req_copy.start()
+    req_copy.wait()
+    for side in (0, 1):
+        for c in range(cap):
+            stage[side, c] = p_loc[jnp.maximum(req_s[side, 1 - side, c], 0)]
+        reply(side).start()
+
+    for copy in index_copies:
+        copy.wait()
+
     @pl.loop(0, shard_rows // 2, unroll=4)
     def _(pair):
         lanes = pl.ds(pl.multiple_of(pair * 128, 128), 128)
         p_turned[:, lanes] = p_loc[pl.ds(pair * 2, 2)].reshape(128, 128).T
 
-    for side in (0, 1):
-        request(side).wait()
-    req_copy = pltpu.make_async_copy(req_v, req_s, local_sem.at[3])
-    req_copy.start()
-    req_copy.wait()
-    for side in (0, 1):
-        for c in range(cap):
-            stage[side, c] = p_loc[jnp.maximum(req_s[side, 1 - side, c], 0)]
-        reply(side).start()
-
-    for copy in index_copies:
-        copy.wait()
-
-    @pl.loop(0, shard_rows // 2)
-    def _(pair):
-        lanes = pl.ds(pl.multiple_of(pair * 128, 128), 128)
-        block = p_turned[:, lanes]
-        owner = lane_pair(agg_ref[pair * 2], agg_ref[pair * 2 + 1], 16)
-        for q in range(grp_count):
-            keep = indicator(owner, q)
-            p_masked[q, :, lanes] = block * jnp.concatenate([keep] * 8, axis=0)
+    def mask_rows(offsets):
+        wanted = [lax.rem(grp + offset, grp_count) for offset in offsets]
+
+        @pl.loop(0, shard_rows // 2, unroll=2)
+        def _(pair):
+            lanes = pl.ds(pl.multiple_of(pair * 128, 128), 128)
+            block = p_turned[:, lanes]
+            owner = lane_pair(agg_ref[pair * 2], agg_ref[pair * 2 + 1], 16)
+            for q in wanted:
+                keep = indicator(owner, q)
+                p_masked[q, :, lanes] = block * jnp.concatenate([keep] * 8, axis=0)
+
+    first_wanted = (half, half + 1, half - 1)
+    mask_rows(first_wanted)
 
     a_copy.wait()
     all_copy.wait()
@@ -151,18 +157,17 @@
             dst_ref=incoming.at[way, step, part, pair],
             send_sem=ring_send.at[way, step, part, pair],
             recv_sem=ring_recv.at[way, step, part, pair],
-            device_id={"grp": (ahead, behind)[way]},
+            device_id={"grp": lax.rem(grp + 1 + way * (grp_count - 2), grp_count)},
             device_id_type=MESH,
         )
 
     def advance(part, step, pair):
-        forth, back = half - step, grp_count - (half - 1 - step)
-        if part == 1:
-            forth, back = grp_count - forth, grp_count - back
-        far, near_by = lax.rem(grp + forth, grp_count), lax.rem(grp + back, grp_count)
+        turn = 1 - 2 * pair
+        far = lax.rem(grp + grp_count + turn * (half - step), grp_count)
+        near_by = lax.rem(grp + grp_count - turn * (half - 1 - step), grp_count)
         left = jnp.concatenate([p_masked[far], p_masked[near_by]], axis=0)
         terms = jnp.dot(left, near[part * 2 + pair], preferred_element_type=jnp.float32)
-        for side, way in ((0, part), (1, 1 - part)):
+        for side, way in ((0, pair), (1, 1 - pair)):
             last = side == 1 and step == half - 1
             if step > 0 and not last:
                 hop(way, step - 1, part, pair).wait_recv()
@@ -187,6 +192,7 @@
     advance(0, 0, 0)
     quarter(1)
     advance(0, 0, 1)
+    mask_rows([offset for offset in range(grp_count) if offset not in first_wanted])
     advance(0, 1, 0)
     quarter(2)
     advance(0, 1, 1)
@@ -205,14 +211,14 @@
 
     for part in (0, 1):
         for pair in (0, 1):
-            hop(part, half - 1, part, pair).wait_recv()
-            hop(1 - part, half - 2, part, pair).wait_recv()
+            hop(pair, half - 1, part, pair).wait_recv()
+            hop(1 - pair, half - 2, part, pair).wait_recv()
             for h in (0, 1):
                 rows = pl.ds((part * 4 + pair * 2 + h) * 128, 128)
                 total_v[rows] = (
                     total_v[rows]
-                    + incoming[part, half - 1, part, pair, h].astype(jnp.float32)
-                    + incoming[1 - part, half - 2, part, pair, h].astype(jnp.float32)
+                    + incoming[pair, half - 1, part, pair, h].astype(jnp.float32)
+                    + incoming[1 - pair, half - 2, part, pair, h].astype(jnp.float32)
                 )
 
     for d in range(128):
@@ -220,7 +226,7 @@
 
     for part in (0, 1):
         for pair in (0, 1):
-            hop(part, half - 1, part, pair).wait_send()
+            hop(pair, half - 1, part, pair).wait_send()
 
 
 def on_device(row_count, grp_count, a_blocks, prolong, a_cols, read_slots, agg, rap_slot):

time: 53.5 us -> 55.4 us (1.036)
  Pallas kernels: 51.5 us -> 53.4 us
    pallas_call x1, Pallas kernels: 51.5 us -> 53.4 us  [on_device(): pl.pallas_call(functools.partial(kernel, row_count, grp_count), out_shape...]
where the time goes in v8:
time: 55.4 us; the launch traced here: 55.3 us
  Pallas kernels  53.4 us (96%)
  local copies, waits for them, and re-layouts  1.87 us (3%)
    pallas_call x1, Pallas kernels, on_device(): pl.pallas_call(functools.partial(kernel, row_count, grp_count), out_shape...  53.4 us
    unnamed x1, local copies, waits for them, and re-layouts  1.87 us

profile of v8, /device:TPU:64, one launch (start us, length us, event | category | flops | bytes accessed | tf_op | source)
XLA Modules:
  0.0 55.3 jit_solution(16260062358052676017)
XLA Ops:
  0.0 53.4 %shard_map.64 = f32[1,8,16384]{2,1,0:T(8,128)} custom-call(s32[2,4]{1,0:T(2,128)} %reads_hbm.1, s32[8,48]{1,0:T(8,128)} %bitcast.2, s32[48]{0:T(128)} %agg_hbm.1, s32[8,48]{1,0:T(8,128)} %bitcast.3, bf16[48,64,512]{2,1,0:T(8,128)(2,1)} %a_hbm.1, bf16[48,64,128]{2,1,0:T(8,128)(2,1)} %p_hbm.1), custom_call_target="tpu_custom_call" | custom-call | tf_op jit(solution)/shard_map/pallas_call | solution.py:241
  53.4 1.9 %copy.8 = f32[1,8,16384]{2,1,0:T(8,128)} copy(f32[1,8,16384]{2,1,0:T(8,128)} %shard_map.64) | data formatting | bytes 1048576

commit v9 on v7

--- a/solution.py
+++ b/solution.py
@@ -113,7 +113,7 @@
     for side in (0, 1):
         reply(side).wait()
 
-    def slot_sums(i, slots):
+    def slot_sums(i, pair):
         columns = jnp.concatenate(
             [p_all[jnp.maximum(cols_ref[k, i], 0)] for k in range(slot_count)], axis=0
         )
@@ -124,7 +124,7 @@
         for k in range(0, slot_count, 2):
             block = a_v[i, :, k * cells : (k + 2) * cells]
             place = lane_pair(places[k], places[k + 1], 16)
-            keeps = [indicator(place, s) for s in slots]
+            keeps = [indicator(place, 2 * pair + h) for h in (0, 1)]
             spread.append(
                 jnp.concatenate(
                     [block * jnp.concatenate([keep] * (cells // 16), axis=0) for keep in keeps],
@@ -135,92 +135,89 @@
             jnp.concatenate(spread, axis=1), columns, preferred_element_type=jnp.float32
         ).astype(jnp.bfloat16)
         rows = pl.ds(pl.multiple_of(i * cells, cells), cells)
-        for n, s in enumerate(slots):
-            near[s // 2, rows, (s % 2) * 128 : (s % 2 + 1) * 128] = product[
-                n * cells : (n + 1) * cells
-            ]
+        for h in (0, 1):
+            near[pair, rows, h * 128 : (h + 1) * 128] = product[h * cells : (h + 1) * cells]
 
     def quarter(pair):
         @pl.loop(0, shard_rows, unroll=min(8, shard_rows))
         def _(i):
-            slot_sums(i, (2 * pair, 2 * pair + 1))
-
-    def hop(way, step, part, pair):
+            slot_sums(i, pair)
+
+    def hop(way, step, pair):
         return pltpu.make_async_remote_copy(
-            src_ref=outgoing.at[way, step, part, pair],
-            dst_ref=incoming.at[way, step, part, pair],
-            send_sem=ring_send.at[way, step, part, pair],
-            recv_sem=ring_recv.at[way, step, part, pair],
-            device_id={"grp": (ahead, behind)[way]},
+            src_ref=outgoing.at[way, step, pair],
+            dst_ref=incoming.at[way, step, pair],
+            send_sem=ring_send.at[way, step, pair],
+            recv_sem=ring_recv.at[way, step, pair],
+            device_id={"grp": lax.rem(grp + 1 + way * (grp_count - 2), grp_count)},
             device_id_type=MESH,
         )
 
-    def advance(part, step, pair):
-        forth, back = half - step, grp_count - (half - 1 - step)
-        if part == 1:
-            forth, back = grp_count - forth, grp_count - back
-        far, near_by = lax.rem(grp + forth, grp_count), lax.rem(grp + back, grp_count)
+    def advance(pair, step, first=False, last=False):
+        long = pair // 2
+        turn = 1 - 2 * long
+        far = lax.rem(grp + grp_count + turn * (half - step), grp_count)
+        near_by = lax.rem(grp + grp_count - turn * (half - 1 - step), grp_count)
         left = jnp.concatenate([p_masked[far], p_masked[near_by]], axis=0)
-        terms = jnp.dot(left, near[part * 2 + pair], preferred_element_type=jnp.float32)
-        for side, way in ((0, part), (1, 1 - part)):
-            last = side == 1 and step == half - 1
-            if step > 0 and not last:
-                hop(way, step - 1, part, pair).wait_recv()
+        terms = jnp.dot(left, near[pair], preferred_element_type=jnp.float32)
+        for side, way in ((0, long), (1, 1 - long)):
+            own = last and side == 1
+            if not first and not own:
+                hop(way, step - 1, pair).wait_recv()
             for h in (0, 1):
                 total = terms[side * 128 : (side + 1) * 128, h * 128 : (h + 1) * 128]
-                if last:
-                    slot = part * 4 + pair * 2 + h
-                    total_v[pl.ds(pl.multiple_of(slot * 128, 128), 128)] = total
+                if own:
+                    total_v[pl.ds(pl.multiple_of((pair * 2 + h) * 128, 128), 128)] = total
                     continue
-                if step > 0:
-                    total = total + incoming[way, step - 1, part, pair, h].astype(jnp.float32)
-                outgoing[way, step, part, pair, h] = total.astype(jnp.bfloat16)
-            if not last:
-                hop(way, step, part, pair).start()
-
-    def advance_both(part, step):
-        @pl.loop(0, 2)
-        def _(pair):
-            advance(part, step, pair)
-
-    quarter(0)
-    advance(0, 0, 0)
-    quarter(1)
-    advance(0, 0, 1)
-    advance(0, 1, 0)
-    quarter(2)
-    advance(0, 1, 1)
-    quarter(3)
-    advance_both(1, 0)
-    for step in range(2, half):
-        advance_both(0, step)
-        advance_both(1, step - 1)
-    advance_both(1, half - 1)
-
-    for way in (0, 1):
-        for step in range(half - 1):
-            for part in (0, 1):
-                for pair in (0, 1):
-                    hop(way, step, part, pair).wait_send()
-
-    for part in (0, 1):
-        for pair in (0, 1):
-            hop(part, half - 1, part, pair).wait_recv()
-            hop(1 - part, half - 2, part, pair).wait_recv()
-            for h in (0, 1):
-                rows = pl.ds((part * 4 + pair * 2 + h) * 128, 128)
-                total_v[rows] = (
-                    total_v[rows]
-                    + incoming[part, half - 1, part, pair, h].astype(jnp.float32)
-                    + incoming[1 - part, half - 2, part, pair, h].astype(jnp.float32)
-                )
+                if not first:
+                    total = total + incoming[way, step - 1, pair, h].astype(jnp.float32)
+                outgoing[way, step, pair, h] = total.astype(jnp.bfloat16)
+            if not own:
+                hop(way, step, pair).start()
+
+    @pl.loop(0, 4)
+    def _(pair):
+        quarter(pair)
+        advance(pair, 0, first=True)
+
+        @pl.loop(1, jnp.minimum(pair, half - 2) + 1)
+        def _(step):
+            advance(pair - step, step)
+
+    advance(0, half - 1, last=True)
+
+    @pl.loop(1, 4)
+    def _(pair):
+        @pl.loop(pair, half - 1)
+        def _(step):
+            advance(3 - (step - pair), step)
+
+        advance(pair, half - 1, last=True)
+
+    @pl.loop(0, 4)
+    def _(pair):
+        long = pair // 2
+
+        @pl.loop(0, half - 1)
+        def _(step):
+            hop(0, step, pair).wait_send()
+            hop(1, step, pair).wait_send()
+
+        hop(long, half - 1, pair).wait_recv()
+        hop(1 - long, half - 2, pair).wait_recv()
+        for h in (0, 1):
+            rows = pl.ds(pl.multiple_of((pair * 2 + h) * 128, 128), 128)
+            total_v[rows] = (
+                total_v[rows]
+                + incoming[long, half - 1, pair, h].astype(jnp.float32)
+                + incoming[1 - long, half - 2, pair, h].astype(jnp.float32)
+            )
 
     for d in range(128):
         out_ref[0, :, d * 128 : (d + 1) * 128] = total_v[pl.ds(d, CSLOT, stride=128)]
 
-    for part in (0, 1):
-        for pair in (0, 1):
-            hop(part, half - 1, part, pair).wait_send()
+    for pair in range(4):
+        hop(pair // 2, half - 1, pair).wait_send()
 
 
 def on_device(row_count, grp_count, a_blocks, prolong, a_cols, read_slots, agg, rap_slot):
@@ -251,15 +248,15 @@
             pltpu.VMEM((2, 2, cap), jnp.int32),
             pltpu.SMEM((2, 2, cap), jnp.int32),
             pltpu.VMEM((2, cap, cells, coarse), b16),
-            pltpu.VMEM((2, half, 2, 2, 2, coarse, coarse), b16),
-            pltpu.VMEM((2, half, 2, 2, 2, coarse, coarse), b16),
+            pltpu.VMEM((2, half, 4, 2, coarse, coarse), b16),
+            pltpu.VMEM((2, half, 4, 2, coarse, coarse), b16),
             dma((7,)),
             dma((2,)),
             dma((2,)),
             dma((2,)),
             dma((2,)),
-            dma((2, half, 2, 2)),
-            dma((2, half, 2, 2)),
+            dma((2, half, 4)),
+            dma((2, half, 4)),
         ],
         compiler_params=pltpu.CompilerParams(
             collective_id=0, has_side_effects=True, vmem_limit_bytes=56 * 1024 * 1024

time: 53.5 us -> 53.1 us (level)
  no operation moved by 1% of the time
where the time goes in v9:
time: 53.1 us; the launch traced here: 53 us
  Pallas kernels  51.1 us (96%)
  local copies, waits for them, and re-layouts  1.87 us (4%)
    pallas_call x1, Pallas kernels, on_device(): pl.pallas_call(functools.partial(kernel, row_count, grp_count), out_shape...  51.1 us
    unnamed x1, local copies, waits for them, and re-layouts  1.87 us

profile of v9, /device:TPU:64, one launch (start us, length us, event | category | flops | bytes accessed | tf_op | source)
XLA Modules:
  0.0 53.0 jit_solution(11311322434393628905)
XLA Ops:
  0.0 51.1 %shard_map.64 = f32[1,8,16384]{2,1,0:T(8,128)} custom-call(s32[2,4]{1,0:T(2,128)} %reads_hbm.1, s32[8,48]{1,0:T(8,128)} %bitcast.2, s32[48]{0:T(128)} %agg_hbm.1, s32[8,48]{1,0:T(8,128)} %bitcast.3, bf16[48,64,512]{2,1,0:T(8,128)(2,1)} %a_hbm.1, bf16[48,64,128]{2,1,0:T(8,128)(2,1)} %p_hbm.1), custom_call_target="tpu_custom_call" | custom-call | tf_op jit(solution)/shard_map/pallas_call | solution.py:232
  51.1 1.9 %copy.8 = f32[1,8,16384]{2,1,0:T(8,128)} copy(f32[1,8,16384]{2,1,0:T(8,128)} %shard_map.64) | data formatting | bytes 1048576

commit v10 on v9

--- a/solution.py
+++ b/solution.py
@@ -99,7 +99,7 @@
     for copy in index_copies:
         copy.wait()
 
-    @pl.loop(0, shard_rows // 2)
+    @pl.loop(0, shard_rows // 2, unroll=4)
     def _(pair):
         lanes = pl.ds(pl.multiple_of(pair * 128, 128), 128)
         block = p_turned[:, lanes]

time: 53.1 us -> 53.1 us (level)
  no operation moved by 1% of the time
where the time goes in v10:
time: 53.1 us; the launch traced here: 53 us
  Pallas kernels  51.1 us (96%)
  local copies, waits for them, and re-layouts  1.87 us (4%)
    pallas_call x1, Pallas kernels, on_device(): pl.pallas_call(functools.partial(kernel, row_count, grp_count), out_shape...  51.1 us
    unnamed x1, local copies, waits for them, and re-layouts  1.87 us

profile of v10, /device:TPU:64, one launch (start us, length us, event | category | flops | bytes accessed | tf_op | source)
XLA Modules:
  0.0 53.0 jit_solution(2358581966355074319)
XLA Ops:
  0.0 51.1 %shard_map.64 = f32[1,8,16384]{2,1,0:T(8,128)} custom-call(s32[2,4]{1,0:T(2,128)} %reads_hbm.1, s32[8,48]{1,0:T(8,128)} %bitcast.2, s32[48]{0:T(128)} %agg_hbm.1, s32[8,48]{1,0:T(8,128)} %bitcast.3, bf16[48,64,512]{2,1,0:T(8,128)(2,1)} %a_hbm.1, bf16[48,64,128]{2,1,0:T(8,128)(2,1)} %p_hbm.1), custom_call_target="tpu_custom_call" | custom-call | tf_op jit(solution)/shard_map/pallas_call | solution.py:232
  51.1 1.9 %copy.8 = f32[1,8,16384]{2,1,0:T(8,128)} copy(f32[1,8,16384]{2,1,0:T(8,128)} %shard_map.64) | data formatting | bytes 1048576
